TPU v7x, 32 devices: a whole 2x2x4 slice. The times are simulated.
32 devices in a mesh: row: 2 (over x), col: 4 (over y, core), depth: 4 (over z).
Axes of the slice: x: 2, y: 2, z: 4, core: 2. Of those that a mesh axis runs over, the one named last changes fastest.
Arguments:
- grad_partial: bfloat16 [4, 8192, 8192], P('depth', 'row', 'col'), may hold values from -6 to 6
- grad_scale: float32 [4, 64, 8192], P('depth', 'row', 'col'), may hold values from 0.01 to 3
- momentum: float32 [8192, 8192], P('row', ('col', 'depth')), may hold values from -6 to 6
Outputs:
- new_momentum: float32 [8192, 8192], P('row', ('col', 'depth'))
- update: float32 [8192, 8192], P('row', ('col', 'depth'))
All inputs are finite; a program needn't handle non-finite values.
Results may differ from a plain program's by a relative error of at most 0.023.
Values may be sent and summed in bfloat16 or wider, within the bound.
A program may use at most 192 MiB of HBM per device.

v0:
```python
import math

import jax
import jax.numpy as jnp
from jax import lax
from jax.sharding import PartitionSpec as P

M = 8192


BETA = 0.95
EPSILON = 1e-07


def from_root(block, axis, owner):
    block = jnp.where(lax.axis_index(axis) == owner, block, jnp.zeros_like(block))
    return lax.psum(block, axis)


def inner_panel(block):
    spread = lax.all_to_all(block, "depth", split_axis=1, concat_axis=1, tiled=True)
    return lax.all_gather(spread, "col", axis=1, tiled=True)


def body(grad_partial, grad_scale, momentum):
    depth_count = lax.axis_size("depth")
    row_count = lax.axis_size("row")
    col_count = lax.axis_size("col")
    rows_blk = grad_partial.shape[1]
    cols_blk = grad_partial.shape[2]
    share_width = cols_blk // depth_count
    piece_width = share_width // depth_count
    groups = grad_scale.shape[1]
    quant_values = grad_partial[0].astype(jnp.float32).reshape(groups, rows_blk // groups, cols_blk)
    scaled = (quant_values * grad_scale[0][:, None, :]).reshape(rows_blk, cols_blk)
    summed_all = lax.psum(scaled.astype(jnp.bfloat16), "depth").astype(jnp.float32)
    gradient = lax.dynamic_slice_in_dim(
        summed_all, lax.axis_index("depth") * share_width, share_width, 1
    )
    new_momentum = BETA * momentum + gradient
    nesterov = gradient + BETA * new_momentum
    total_sq = lax.psum(jnp.sum(nesterov * nesterov), ("row", "col", "depth"))
    ortho_input = (nesterov * (math.sqrt(M) / (1.5 * (jnp.sqrt(total_sq) + EPSILON)))).astype(
        jnp.bfloat16
    )
    left_panel = inner_panel(ortho_input)
    taken_rows = min(rows_blk, cols_blk)
    col_index = lax.axis_index("col")
    offset = col_index * cols_blk % rows_blk
    first_root = col_index * cols_blk // rows_blk
    own_rows = lax.dynamic_slice_in_dim(left_panel, offset, taken_rows, 0)
    block_terms = []
    for root_step in range(max(1, row_count // col_count)):
        arrived = from_root(own_rows, "row", first_root + root_step)
        block_terms.append(
            lax.dot_general(
                left_panel, arrived, (((1,), (1,)), ((), ())), preferred_element_type=jnp.float32
            )
        )
    partial_value = jnp.concatenate(block_terms, axis=1)
    rounded = lax.optimization_barrier(partial_value.astype(jnp.bfloat16)).astype(jnp.float32)
    gram_matrix = lax.psum_scatter(
        rounded.astype(jnp.bfloat16), "depth", scatter_dimension=1, tiled=True
    )
    left_gram = inner_panel(gram_matrix)
    stacked = ortho_input.reshape(rows_blk // share_width, depth_count, piece_width, share_width)
    exchanged = lax.all_to_all(stacked, "depth", split_axis=1, concat_axis=3, tiled=True)
    rows_part = exchanged.reshape(rows_blk // depth_count, cols_blk)
    summed = jnp.dot(
        left_gram,
        lax.all_gather(rows_part, "row", axis=0, tiled=True),
        preferred_element_type=jnp.float32,
    )
    product = lax.psum_scatter(
        summed.astype(jnp.bfloat16), "depth", scatter_dimension=1, tiled=True
    ).astype(jnp.float32)
    update = math.sqrt(M) * (1.5 * ortho_input.astype(jnp.float32) - 0.5 * product)
    return (new_momentum, update)


def solution(mesh):
    placed = (P("depth", "row", "col"), P("depth", "row", "col"), P("row", ("col", "depth")))
    return jax.shard_map(
        body,
        mesh=mesh,
        in_specs=placed,
        out_specs=(P("row", ("col", "depth")), P("row", ("col", "depth"))),
        check_vma=False,
    )
```

profile of v0, /device:TPU:0, one launch (start us, length us, event | category | flops | bytes accessed | tf_op | source)
XLA Modules:
  0.0 2021.6 jit_solution(17645372359974030297)
XLA Ops:
  7.2 0.0 all-reduce.3.cloned.1.call-start
  7.2 14.9 fusion
  22.1 0.0 all-gather.4.cloned.1.call-start
  22.2 565.0 %all-reduce.3.cloned.1.call-done = bf16[4096,2048]{1,0:T(8,128)(2,1)} async-done(((bf16[4096,2048]{1,0:T(8,128)(2,1)}), bf16[4096,2048]{1,0:T(8,128)(2,1)}) %all-reduce.3.cloned.1.call-update) | async-done | bytes 16777232 | tf_op jit(solution)/shard_map/psum | solution.py:36
  587.1 8.3 multiply_reduce_fusion
  595.5 39.4 %psum.22 = f32[]{:T(128)} all-reduce(f32[]{:T(128)} %get-tuple-element.2), channel_id=1, replica_groups=mesh['row'=2,'col'=4,'depth'=4] {'row','col','depth'}, use_global_device_ids=true, to_apply=%region_2.0 | all-reduce | flops 1 | bytes 8 | tf_op jit(solution)/shard_map/psum | solution.py:42
  635.6 6.1 multiply_convert_fusion
  641.7 1.9 copy-done
  643.6 0.7 copy_bitcast_fusion.2
  644.3 96.2 %all_to_all.39 = bf16[4096,4,128]{2,0,1:T(8,128)(2,1)} all-to-all(bf16[4096,4,128]{2,0,1:T(8,128)(2,1)S(1)} %copy_bitcast_fusion.2), channel_id=1, replica_groups=mesh['row'=2,'col'=4,'depth'=4] {'depth'}, dimensions={1} | all-to-all | bytes 8388608 | tf_op jit(solution)/shard_map/all_to_all | solution.py:21
  740.5 6.3 copy.10
  746.9 0.0 all-reduce.5.cloned.1.call-start
  747.0 104.9 %all-gather.4.cloned.1.call-done = bf16[4096,2048]{0,1:T(8,128)(2,1)} async-done(((bf16[4096,512]{0,1:T(8,128)(2,1)}), bf16[4096,2048]{0,1:T(8,128)(2,1)}) %all-gather.4.cloned.1.call-update) | async-done | bytes 16777232 | tf_op jit(solution)/shard_map/all_gather | solution.py:22
  851.9 9.9 dynamic-slice_select_fusion
  861.8 0.0 reduce-scatter.3.cloned.1.call-start
  861.8 198.1 %all-reduce.5.cloned.1.call-done = bf16[2048,2048]{0,1:T(8,128)(2,1)} async-done(((bf16[2048,2048]{0,1:T(8,128)(2,1)}), bf16[2048,2048]{0,1:T(8,128)(2,1)}) %all-reduce.5.cloned.1.call-update) | async-done | bytes 8388624 | tf_op jit(solution)/shard_map/psum | solution.py:17
  1059.9 42.0 %convolution_convert_fusion.1 = bf16[4096,2048]{1,0:T(8,128)(2,1)} fusion(bf16[4096,2048]{0,1:T(8,128)(2,1)} %all-gather.4.cloned.1.call-done, bf16[2048,2048]{0,1:T(8,128)(2,1)} %all-reduce.5.cloned.1.call-done), kind=kOutput, calls=%fused_computation.3 | convolution fusion | flops 34368126976 | bytes 41943040 | tf_op jit(solution)/shard_map/dot_general | solution.py:56
  1101.9 0.2 all-gather.8.cloned.1.call-start
  1102.2 7.8 copy.13
  1110.0 207.3 %all_to_all.40 = bf16[8,4,128,512]{2,0,3,1:T(8,128)(2,1)S(1)} all-to-all(bf16[8,4,128,512]{2,0,3,1:T(8,128)(2,1)} %copy.13), channel_id=1, replica_groups=mesh['row'=2,'col'=4,'depth'=4] {'depth'}, dimensions={1} | all-to-all | bytes 8388608 | tf_op jit(solution)/shard_map/all_to_all | solution.py:67
  1317.3 3.0 copy.20
  1320.3 0.0 all-gather.6.cloned.1.call-start
  1320.4 145.1 %reduce-scatter.3.cloned.1.call-done = bf16[4096,512]{1,0:T(8,128)(2,1)} async-done(((bf16[4096,2048]{1,0:T(8,128)(2,1)}), bf16[4096,512]{1,0:T(8,128)(2,1)}) %reduce-scatter.3.cloned.1.call-update) | async-done | bytes 4194320 | tf_op jit(solution)/shard_map/reduce_scatter | solution.py:62
  1465.5 2.9 copy_bitcast_fusion.1
  1468.4 101.7 %all_to_all.41 = bf16[4096,4,128]{2,0,1:T(8,128)(2,1)} all-to-all(bf16[4096,4,128]{2,0,1:T(8,128)(2,1)S(1)} %copy_bitcast_fusion.1), channel_id=1, replica_groups=mesh['row'=2,'col'=4,'depth'=4] {'depth'}, dimensions={1} | all-to-all | bytes 8388608 | tf_op jit(solution)/shard_map/all_to_all | solution.py:21
  1570.1 6.3 copy.12
  1576.5 0.0 reduce-scatter.5.cloned.1.call-start
  1576.5 0.0 all-gather.8.cloned.1.call-done
  1576.5 107.4 %all-gather.6.cloned.1.call-done = bf16[4096,2048]{0,1:T(8,128)(2,1)} async-done(((bf16[4096,512]{0,1:T(8,128)(2,1)}), bf16[4096,2048]{0,1:T(8,128)(2,1)}) %all-gather.6.cloned.1.call-update) | async-done | bytes 16777232 | tf_op jit(solution)/shard_map/all_gather | solution.py:22
  1683.9 41.9 %convolution_convert_fusion = bf16[4096,2048]{1,0:T(8,128)(2,1)} fusion(bf16[4096,2048]{0,1:T(8,128)(2,1)} %all-gather.6.cloned.1.call-done, bf16[2048,2048]{0,1:T(8,128)(2,1)} %all-gather.8.cloned.1.call-done), kind=kOutput, calls=%fused_computation.2 | convolution fusion | flops 34368126976 | bytes 41943040 | tf_op jit(solution)/shard_map/dot_general | solution.py:69
  1725.8 280.5 %reduce-scatter.5.cloned.1.call-done = bf16[4096,512]{1,0:T(8,128)(2,1)} async-done(((bf16[4096,2048]{1,0:T(8,128)(2,1)}), bf16[4096,512]{1,0:T(8,128)(2,1)}) %reduce-scatter.5.cloned.1.call-update) | async-done | bytes 4194320 | tf_op jit(solution)/shard_map/reduce_scatter | solution.py:74
  2006.3 8.5 subtract_multiply_fusion
  (8 shorter events, 0.1 us)
Async XLA Ops:
  7.2 580.0 %all-reduce.3.cloned.1.call-start = ((), (), s32[]{:S(2)}) async-start(), calls=%async_computation.5 | async-start | bytes 33554432 | tf_op jit(solution)/shard_map/psum | solution.py:36
  22.1 829.8 %all-gather.4.cloned.1.call-start = ((), (), s32[]{:S(2)}) async-start(), calls=%async_computation.6 | async-start | bytes 20971520 | tf_op jit(solution)/shard_map/all_gather | solution.py:22
  641.7 1.9 copy-start
  746.9 313.1 %all-reduce.5.cloned.1.call-start = ((), (), s32[]{:S(2)}) async-start(), calls=%async_computation.7 | async-start | bytes 16777216 | tf_op jit(solution)/shard_map/psum | solution.py:17
  861.8 603.7 %reduce-scatter.3.cloned.1.call-start = ((), (), s32[]{:S(2)}) async-start(), calls=%async_computation.8 | async-start | bytes 20971520 | tf_op jit(solution)/shard_map/reduce_scatter | solution.py:62
  1101.9 474.6 %all-gather.8.cloned.1.call-start = ((), (), s32[]{:S(2)}) async-start(), calls=%async_computation.10 | async-start | bytes 12582912 | tf_op jit(solution)/shard_map/all_gather | solution.py:71
  1320.3 363.6 %all-gather.6.cloned.1.call-start = ((), (), s32[]{:S(2)}) async-start(), calls=%async_computation.9 | async-start | bytes 20971520 | tf_op jit(solution)/shard_map/all_gather | solution.py:22
  1576.5 429.8 %reduce-scatter.5.cloned.1.call-start = ((), (), s32[]{:S(2)}) async-start(), calls=%async_computation.11 | async-start | bytes 20971520 | tf_op jit(solution)/shard_map/reduce_scatter | solution.py:74
Sparse Core Ops, SparseCore 0:
  22.2 564.8 all-reduce.2
  747.0 104.8 all-gather.3
  861.9 197.9 all-reduce.4
  1102.1 363.3 reduce-scatter.2
  1466.9 108.9 all-gather.7
  1578.0 105.9 all-gather.5
  1725.9 280.2 reduce-scatter.4
where the time goes:
time: 2020 us
  waiting for transfers between devices  1400 us (69%)
  blocking collectives  445 us (22%)
  matrix products  83.8 us (4%)
  other arithmetic  47.6 us (2%)
  local copies, waits for them, and re-layouts  29 us (1%)
    psum x1, waiting for transfers between devices, body(): lax.psum(scaled.astype(jnp.bfloat16), 'depth').astype(jnp.float32)  565 us
    reduce_scatter x1, waiting for transfers between devices, body(): lax.psum_scatter(summed.astype(jnp.bfloat16), 'depth', scatter_dimension=...  280 us
    all_gather x2, waiting for transfers between devices, inner_panel(): return lax.all_gather(spread, 'col', axis=1, tiled=True)  212 us
    all_to_all x1, blocking collectives, body(): lax.all_to_all(stacked, 'depth', split_axis=1, concat_axis=3, tiled=True)  207 us
    psum x1, waiting for transfers between devices, from_root(): return lax.psum(block, axis)  198 us
    all_to_all x2, blocking collectives, inner_panel(): lax.all_to_all(block, 'depth', split_axis=1, concat_axis=1, tiled=True)  198 us
    reduce_scatter x1, waiting for transfers between devices, body(): lax.psum_scatter(rounded.astype(jnp.bfloat16), 'depth', scatter_dimension...  145 us
    dot_general x1, matrix products, body(): lax.dot_general(left_panel, arrived, (((1,), (1,)), ((), ())), preferred_...  42 us
  transfers between devices with their start and end apart: 7, of which 6 were waited for; matrix products, arithmetic and copies ran while one was open for 1% of the time, Pallas kernels for 0%

commit v1 on v0

v1 whole, which is shorter than its diff:
```python
import math

import jax
import jax.numpy as jnp
from jax import lax
from jax.sharding import PartitionSpec as P

M = 8192
BETA = 0.95
EPSILON = 1e-07
PIECES = 4


def row_sum(block):
    if lax.axis_size("row") != 2:
        return lax.psum(block.astype(jnp.bfloat16), "row").astype(jnp.float32)
    moved = lax.ppermute(block.astype(jnp.bfloat16), "row", [(0, 1), (1, 0)])
    return block.astype(jnp.float32) + moved.astype(jnp.float32)


def body(grad_partial, grad_scale, momentum):
    depth_count = lax.axis_size("depth")
    rows_blk, cols_blk = grad_partial.shape[1:]
    share = cols_blk // depth_count
    width = share // PIECES
    groups = grad_scale.shape[1]
    group_rows = rows_blk // groups

    def scaled_piece(start):
        quant = lax.slice_in_dim(grad_partial[0], start, start + width, axis=1)
        scale = lax.slice_in_dim(grad_scale[0], start, start + width, axis=1)
        quant = quant.astype(jnp.float32).reshape(groups, group_rows, width)
        return (quant * scale[:, None, :]).reshape(rows_blk, width).astype(jnp.bfloat16)

    sums = []
    for j in range(PIECES):
        scaled = jnp.stack([scaled_piece(z * share + j * width) for z in range(depth_count)])
        scaled = lax.optimization_barrier(scaled)
        sums.append(lax.psum_scatter(scaled, "depth", scatter_dimension=0))

    momenta, mine, squares = [], [], []
    for j in range(PIECES):
        gradient = sums[j]
        if mine:
            gradient, mine[-1] = lax.optimization_barrier((gradient, mine[-1]))
        gradient = gradient.astype(jnp.float32)
        new = BETA * lax.slice_in_dim(momentum, j * width, (j + 1) * width, axis=1) + gradient
        nesterov = gradient + BETA * new
        new, kept, square = lax.optimization_barrier(
            (new, nesterov.astype(jnp.bfloat16), jnp.sum(nesterov * nesterov))
        )
        momenta.append(new)
        mine.append(kept)
        squares.append(square)
    total_sq = lax.psum(sum(squares), ("row", "col", "depth"))
    factor = math.sqrt(M) / (1.5 * (jnp.sqrt(total_sq) + EPSILON))
    own = jnp.concatenate(mine, axis=1)

    product = None
    for j in range(PIECES):
        panel = lax.all_gather(mine[j], ("col", "depth"), axis=1, tiled=True)
        gram = lax.dot_general(
            panel, own, (((0,), (0,)), ((), ())), preferred_element_type=jnp.float32
        )
        gram = row_sum(gram.astype(jnp.bfloat16))
        gram = (gram * (factor * factor)).astype(jnp.bfloat16)
        term = jnp.dot(panel, gram, preferred_element_type=jnp.float32)
        product = term if product is None else product + term
    update = (math.sqrt(M) * factor) * (1.5 * own.astype(jnp.float32) - 0.5 * product)
    return (jnp.concatenate(momenta, axis=1), update)


def solution(mesh):
    placed = (P("depth", "row", "col"), P("depth", "row", "col"), P("row", ("col", "depth")))
    return jax.shard_map(
        body,
        mesh=mesh,
        in_specs=placed,
        out_specs=(P("row", ("col", "depth")), P("row", ("col", "depth"))),
        check_vma=False,
    )
```

time: 2020 us -> 969 us (0.48)
  waiting for transfers between devices: 1400 us -> 706 us
  blocking collectives: 445 us -> 46.6 us
  matrix products: 83.8 us -> 128 us
    psum x2 -> x0, waiting for transfers between devices: 763 us -> none  [the longest x1 565 us: body(): lax.psum(scaled.astype(jnp.bfloat16), 'depth').astype(jnp.float32)]
    all_to_all x3 -> x0, blocking collectives: 405 us -> none  [the longest x1 207 us: body(): lax.all_to_all(stacked, 'depth', split_axis=1, concat_axis=3, tiled=True)]
    all_gather x3 -> x4, waiting for transfers between devices: 212 us -> 413 us  [body(): panel = lax.all_gather(mine[j], ('col', 'depth'), axis=1, tiled=True)]
    reduce_scatter x2 -> x4, waiting for transfers between devices: 426 us -> 291 us  [body(): sums.append(lax.psum_scatter(scaled, 'depth', scatter_dimension=0))]
    dot_general x2 -> x8, matrix products: 83.8 us -> 128 us  [the longest x4 71.4 us: body(): term = jnp.dot(panel, gram, preferred_element_type=jnp.float32)]
  transfers between devices with their start and end apart: 7 -> 12, of which waited for: 6 -> 9; matrix products, arithmetic and copies ran while one was open for 1% -> 15% of each run, Pallas kernels for 0% -> 0%
where the time goes in v1:
time: 969 us; the launch traced here: 964 us
  waiting for transfers between devices  706 us (73%)
  matrix products  128 us (13%)
  other arithmetic  49 us (5%)
  blocking collectives  46.6 us (5%)
  between operations  18 us (2%)
  local copies, waits for them, and re-layouts  10.1 us (1%)
    all_gather x4, waiting for transfers between devices, body(): panel = lax.all_gather(mine[j], ('col', 'depth'), axis=1, tiled=True)  413 us
    reduce_scatter x4, waiting for transfers between devices, body(): sums.append(lax.psum_scatter(scaled, 'depth', scatter_dimension=0))  291 us
    dot_general x4, matrix products, body(): term = jnp.dot(panel, gram, preferred_element_type=jnp.float32)  71.4 us
    dot_general x4, matrix products, body(): lax.dot_general(panel, own, (((0,), (0,)), ((), ())), preferred_element_t...  56.9 us
    psum x1, blocking collectives, body(): total_sq = lax.psum(sum(squares), ('row', 'col', 'depth'))  46.6 us
  transfers between devices with their start and end apart: 12, of which 9 were waited for; matrix products, arithmetic and copies ran while one was open for 15% of the time, Pallas kernels for 0%

profile of v1, /device:TPU:0, one launch (start us, length us, event | category | flops | bytes accessed | tf_op | source)
XLA Modules:
  0.0 964.0 jit_solution(6642222511365399788)
XLA Ops:
  8.1 4.8 fusion.17
  13.0 7.7 fusion.18
  20.6 2.4 pad_maximum_fusion.1
  23.1 3.3 pad_maximum_fusion.2
  28.2 3.3 pad_maximum_fusion.3
  33.8 3.3 pad_maximum_fusion.4
  37.2 65.4 %reduce-scatter.5.cloned.1.call-done = bf16[1,4096,128]{2,1,0:T(8,128)(2,1)} async-done(((bf16[4,4096,128]{2,1,0:T(8,128)(2,1)}), bf16[1,4096,128]{2,1,0:T(8,128)(2,1)}) %reduce-scatter.5.cloned.1.call-update) | async-done | bytes 1048592 | tf_op jit(solution)/shard_map/reduce_scatter | solution.py:39
  102.6 4.8 multiply_reduce_fusion.3
  107.4 74.9 %reduce-scatter.7.cloned.1.call-done = bf16[1,4096,128]{2,1,0:T(8,128)(2,1)} async-done(((bf16[4,4096,128]{2,1,0:T(8,128)(2,1)}), bf16[1,4096,128]{2,1,0:T(8,128)(2,1)}) %reduce-scatter.7.cloned.1.call-update) | async-done | bytes 1048592 | tf_op jit(solution)/shard_map/reduce_scatter | solution.py:39
  182.3 4.8 multiply_reduce_fusion.2
  187.1 75.4 %reduce-scatter.9.cloned.1.call-done = bf16[1,4096,128]{2,1,0:T(8,128)(2,1)} async-done(((bf16[4,4096,128]{2,1,0:T(8,128)(2,1)}), bf16[1,4096,128]{2,1,0:T(8,128)(2,1)}) %reduce-scatter.9.cloned.1.call-update) | async-done | bytes 1048592 | tf_op jit(solution)/shard_map/reduce_scatter | solution.py:39
  262.5 4.8 multiply_reduce_fusion.1
  267.3 75.3 %reduce-scatter.11.cloned.1.call-done = bf16[1,4096,128]{2,1,0:T(8,128)(2,1)} async-done(((bf16[4,4096,128]{2,1,0:T(8,128)(2,1)}), bf16[1,4096,128]{2,1,0:T(8,128)(2,1)}) %reduce-scatter.11.cloned.1.call-update) | async-done | bytes 1048592 | tf_op jit(solution)/shard_map/reduce_scatter | solution.py:39
  344.0 4.8 multiply_reduce_fusion
  351.6 46.6 %psum.7 = f32[]{:T(128)} all-reduce(f32[]{:T(128)S(6)} %add.77), channel_id=1, replica_groups=mesh['row'=2,'col'=4,'depth'=4] {'row','col','depth'}, use_global_device_ids=true, to_apply=%region_8.0 | all-reduce | flops 1 | bytes 8 | tf_op jit(solution)/shard_map/psum | solution.py:55
  404.1 4.9 pad_maximum_fusion
  409.0 68.3 %all-gather.9.cloned.1.call-done = bf16[4096,2048]{1,0:T(8,128)(2,1)} async-done(((bf16[4096,128]{1,0:T(8,128)(2,1)}), bf16[4096,2048]{1,0:T(8,128)(2,1)}) %all-gather.9.cloned.1.call-update) | async-done | bytes 16777232 | tf_op jit(solution)/shard_map/all_gather | solution.py:61
  477.3 13.6 %convolution_convert_fusion.1 = bf16[2048,512]{1,0:T(8,128)(2,1)S(1)} fusion(bf16[4096,2048]{1,0:T(8,128)(2,1)} %all-gather.9.cloned.1.call-done, bf16[4096,512]{1,0:T(8,128)(2,1)} %constant_dynamic-update-slice_fusion), kind=kOutput, calls=%fused_computation.11 | convolution fusion | flops 8590983168 | bytes 23068672 | tf_op jit(solution)/shard_map/dot_general | solution.py:62
  491.0 1.5 collective-permute-start.2
  492.5 115.3 %all-gather.5.cloned.1.call-done = bf16[4096,2048]{1,0:T(8,128)(2,1)} async-done(((bf16[4096,128]{1,0:T(8,128)(2,1)}), bf16[4096,2048]{1,0:T(8,128)(2,1)}) %all-gather.5.cloned.1.call-update) | async-done | bytes 16777232 | tf_op jit(solution)/shard_map/all_gather | solution.py:61
  607.8 14.6 %convolution_convert_fusion.3 = bf16[2048,512]{1,0:T(8,128)(2,1)} fusion(bf16[4096,2048]{1,0:T(8,128)(2,1)} %all-gather.5.cloned.1.call-done, bf16[4096,512]{1,0:T(8,128)(2,1)} %constant_dynamic-update-slice_fusion), kind=kOutput, calls=%fused_computation.13 | convolution fusion | flops 8590983168 | bytes 23068672 | tf_op jit(solution)/shard_map/dot_general | solution.py:62
  622.4 1.5 collective-permute-start
  623.9 114.5 %all-gather.7.cloned.1.call-done = bf16[4096,2048]{1,0:T(8,128)(2,1)} async-done(((bf16[4096,128]{1,0:T(8,128)(2,1)}), bf16[4096,2048]{1,0:T(8,128)(2,1)}) %all-gather.7.cloned.1.call-update) | async-done | bytes 16777232 | tf_op jit(solution)/shard_map/all_gather | solution.py:61
  738.4 14.7 %convolution_convert_fusion.2 = bf16[2048,512]{1,0:T(8,128)(2,1)} fusion(bf16[4096,2048]{1,0:T(8,128)(2,1)} %all-gather.7.cloned.1.call-done, bf16[4096,512]{1,0:T(8,128)(2,1)} %constant_dynamic-update-slice_fusion), kind=kOutput, calls=%fused_computation.12 | convolution fusion | flops 8590983168 | bytes 23068672 | tf_op jit(solution)/shard_map/dot_general | solution.py:62
  753.1 1.5 collective-permute-start.1
  754.6 114.5 %all-gather.11.cloned.1.call-done = bf16[4096,2048]{1,0:T(8,128)(2,1)} async-done(((bf16[4096,128]{1,0:T(8,128)(2,1)}), bf16[4096,2048]{1,0:T(8,128)(2,1)}) %all-gather.11.cloned.1.call-update) | async-done | bytes 16777232 | tf_op jit(solution)/shard_map/all_gather | solution.py:61
  869.0 13.9 %convolution_convert_fusion = bf16[2048,512]{1,0:T(8,128)(2,1)S(1)} fusion(bf16[4096,2048]{1,0:T(8,128)(2,1)} %all-gather.11.cloned.1.call-done, bf16[4096,512]{1,0:T(8,128)(2,1)} %constant_dynamic-update-slice_fusion), kind=kOutput, calls=%fused_computation.10 | convolution fusion | flops 8590983168 | bytes 23068672 | tf_op jit(solution)/shard_map/dot_general | solution.py:62
  883.0 1.5 collective-permute-start.3
  884.6 15.9 %fusion.2 = f32[4096,512]{1,0:T(8,128)} fusion(bf16[4096,2048]{1,0:T(8,128)(2,1)} %all-gather.9.cloned.1.call-done, bf16[2048,512]{1,0:T(8,128)(2,1)} %collective-permute-done.2, bf16[2048,512]{1,0:T(8,128)(2,1)S(1)} %convolution_convert_fusion.1, f32[]{:T(128)S(6)} %mul.325), kind=kOutput, calls=%fused_computation.24 | convolution fusion | flops 8595177472 | bytes 29360132 | tf_op jit(solution)/shard_map/dot_general | solution.py:67
  900.6 13.8 %fusion = f32[4096,512]{1,0:T(8,128)} fusion(bf16[4096,2048]{1,0:T(8,128)(2,1)S(1)} %bitcast.129, bf16[2048,512]{1,0:T(8,128)(2,1)} %collective-permute-done, bf16[2048,512]{1,0:T(8,128)(2,1)} %convolution_convert_fusion.3, f32[]{:T(128)S(6)} %mul.325), kind=kOutput, calls=%fused_computation.22 | convolution fusion | flops 8595177472 | bytes 29360132 | tf_op jit(solution)/shard_map/dot_general | solution.py:67
  914.3 15.9 %fusion.1 = f32[4096,512]{1,0:T(8,128)} fusion(bf16[4096,2048]{1,0:T(8,128)(2,1)} %all-gather.7.cloned.1.call-done, bf16[2048,512]{1,0:T(8,128)(2,1)} %collective-permute-done.1, bf16[2048,512]{1,0:T(8,128)(2,1)} %convolution_convert_fusion.2, f32[]{:T(128)S(6)} %mul.325), kind=kOutput, calls=%fused_computation.23 | convolution fusion | flops 8595177472 | bytes 29360132 | tf_op jit(solution)/shard_map/dot_general | solution.py:67
  931.0 25.9 %subtract_multiply_fusion = f32[4096,512]{1,0:T(8,128)} fusion(f32[4096,512]{1,0:T(8,128)} %fusion.2, f32[4096,512]{1,0:T(8,128)} %fusion, f32[4096,512]{1,0:T(8,128)} %fusion.1, bf16[4096,512]{1,0:T(8,128)(2,1)} %constant_dynamic-update-slice_fusion, bf16[4096,2048]{1,0:T(8,128)(2,1)} %all-gather.11.cloned.1.call-done, f32[]{:T(128)S(6)} %mul.321, ...), kind=kOutput, calls=%fused_computation.1 | convolution fusion | flops 8611954688 | bytes 58720264 | tf_op jit(solution)/shard_map/dot_general | solution.py:67
  (64 shorter events, 12.5 us)
Async XLA Ops:
  7.2 95.5 %reduce-scatter.5.cloned.1.call-start = ((), (), s32[]{:S(2)}) async-start(), calls=%async_computation.4 | async-start | bytes 5242880 | tf_op jit(solution)/shard_map/reduce_scatter | solution.py:39
  23.0 159.3 %reduce-scatter.7.cloned.1.call-start = ((), (), s32[]{:S(2)}) async-start(), calls=%async_computation.5 | async-start | bytes 5242880 | tf_op jit(solution)/shard_map/reduce_scatter | solution.py:39
  26.4 1.2 copy-start.10
  26.4 1.5 copy-start.11
  26.4 1.9 copy-start.12
  26.4 236.1 %reduce-scatter.9.cloned.1.call-start = ((), (), s32[]{:S(2)}) async-start(), calls=%async_computation.6 | async-start | bytes 5242880 | tf_op jit(solution)/shard_map/reduce_scatter | solution.py:39
  31.5 1.5 copy-start.7
  31.5 1.9 copy-start.8
  31.5 2.3 copy-start.9
  31.6 311.0 %reduce-scatter.11.cloned.1.call-start = ((), (), s32[]{:S(2)}) async-start(), calls=%async_computation.7 | async-start | bytes 5242880 | tf_op jit(solution)/shard_map/reduce_scatter | solution.py:39
  37.2 440.1 %all-gather.9.cloned.1.call-start = ((), (), s32[]{:S(2)}) async-start(), calls=%async_computation.10 | async-start | bytes 17825792 | tf_op jit(solution)/shard_map/all_gather | solution.py:61
  342.6 265.2 %all-gather.5.cloned.1.call-start = ((), (), s32[]{:S(2)}) async-start(), calls=%async_computation.8 | async-start | bytes 17825792 | tf_op jit(solution)/shard_map/all_gather | solution.py:61
  343.2 55.7 %copy-start = (bf16[4096,128]{1,0:T(8,128)(2,1)S(1)}, bf16[4096,128]{1,0:T(8,128)(2,1)}, u32[]{:S(2)}) copy-start(bf16[4096,128]{1,0:T(8,128)(2,1)} %get-tuple-element.34) | copy-start | bytes 3145732
  343.2 395.2 %all-gather.7.cloned.1.call-start = ((), (), s32[]{:S(2)}) async-start(), calls=%async_computation.9 | async-start | bytes 17825792 | tf_op jit(solution)/shard_map/all_gather | solution.py:61
  344.0 56.1 %copy-start.1 = (bf16[4096,128]{1,0:T(8,128)(2,1)S(1)}, bf16[4096,128]{1,0:T(8,128)(2,1)}, u32[]{:S(2)}) copy-start(bf16[4096,128]{1,0:T(8,128)(2,1)} %get-tuple-element.35) | copy-start | bytes 3145732
  344.0 525.1 %all-gather.11.cloned.1.call-start = ((), (), s32[]{:S(2)}) async-start(), calls=%async_computation.11 | async-start | bytes 17825792 | tf_op jit(solution)/shard_map/all_gather | solution.py:61
  348.9 52.4 %copy-start.2 = (bf16[4096,128]{1,0:T(8,128)(2,1)S(1)}, bf16[4096,128]{1,0:T(8,128)(2,1)}, u32[]{:S(2)}) copy-start(bf16[4096,128]{1,0:T(8,128)(2,1)} %get-tuple-element.36) | copy-start | bytes 3145732
  398.9 3.5 copy-start.3
  398.9 4.6 copy-start.4
  398.9 4.6 copy-start.5
  398.9 5.2 copy-start.6
  491.0 393.6 %collective-permute-start.2 = (bf16[2048,512]{1,0:T(8,128)(2,1)S(1)}, bf16[2048,512]{1,0:T(8,128)(2,1)}, u32[]{:S(2)}, u32[]{:S(2)}) collective-permute-start(bf16[2048,512]{1,0:T(8,128)(2,1)S(1)} %convolution_convert_fusion.1), channel_id=1, source_target_pairs={{0,16},{16,0},{1,17},{17,1},{2,18},{18,2},{3,19},{19,3},{4,20},{20... | collective-permute-start | bytes 6291464 | tf_op jit(solution)/shard_map/ppermute | solution.py:17
  622.4 278.1 %collective-permute-start = (bf16[2048,512]{1,0:T(8,128)(2,1)}, bf16[2048,512]{1,0:T(8,128)(2,1)}, u32[]{:S(2)}, u32[]{:S(2)}) collective-permute-start(bf16[2048,512]{1,0:T(8,128)(2,1)} %convolution_convert_fusion.3), channel_id=1, source_target_pairs={{0,16},{16,0},{1,17},{17,1},{2,18},{18,2},{3,19},{19,3},{4,20},{20... | collective-permute-start | bytes 6291464 | tf_op jit(solution)/shard_map/ppermute | solution.py:17
  753.1 161.3 %collective-permute-start.1 = (bf16[2048,512]{1,0:T(8,128)(2,1)}, bf16[2048,512]{1,0:T(8,128)(2,1)}, u32[]{:S(2)}, u32[]{:S(2)}) collective-permute-start(bf16[2048,512]{1,0:T(8,128)(2,1)} %convolution_convert_fusion.2), channel_id=1, source_target_pairs={{0,16},{16,0},{1,17},{17,1},{2,18},{18,2},{3,19},{19,3},{4,20},{20... | collective-permute-start | bytes 6291464 | tf_op jit(solution)/shard_map/ppermute | solution.py:17
  869.0 31.5 %slice-start = ((s8[16777216]{0:T(1024)(128)(4,1)}), s8[4194304]{0:T(1024)(128)(4,1)S(1)}, s32[]{:S(2)}) async-start(s8[16777216]{0:T(1024)(128)(4,1)} %bitcast.128), calls=%async_computation.12 | async-start | bytes 8388608
  869.0 31.5 %slice-start.1 = ((s8[16777216]{0:T(1024)(128)(4,1)}), s8[4194304]{0:T(1024)(128)(4,1)S(1)}, s32[]{:S(2)}) async-start(s8[16777216]{0:T(1024)(128)(4,1)} %bitcast.128), calls=%async_computation.13 | async-start | bytes 8388608
  883.0 17.5 %copy-start.13 = (bf16[2048,512]{1,0:T(8,128)(2,1)}, bf16[2048,512]{1,0:T(8,128)(2,1)S(1)}, u32[]{:S(2)}) copy-start(bf16[2048,512]{1,0:T(8,128)(2,1)S(1)} %convolution_convert_fusion) | copy-start | bytes 6291460
  883.0 17.5 %slice-start.2 = ((s8[16777216]{0:T(1024)(128)(4,1)}), s8[4194304]{0:T(1024)(128)(4,1)S(1)}, s32[]{:S(2)}) async-start(s8[16777216]{0:T(1024)(128)(4,1)} %bitcast.128), calls=%async_computation.14 | async-start | bytes 8388608
  883.0 17.5 %slice-start.3 = ((s8[16777216]{0:T(1024)(128)(4,1)}), s8[4194304]{0:T(1024)(128)(4,1)S(1)}, s32[]{:S(2)}) async-start(s8[16777216]{0:T(1024)(128)(4,1)} %bitcast.128), calls=%async_computation.15 | async-start | bytes 8388608
  883.0 48.0 %collective-permute-start.3 = (bf16[2048,512]{1,0:T(8,128)(2,1)S(1)}, bf16[2048,512]{1,0:T(8,128)(2,1)}, u32[]{:S(2)}, u32[]{:S(2)}) collective-permute-start(bf16[2048,512]{1,0:T(8,128)(2,1)S(1)} %convolution_convert_fusion), channel_id=1, source_target_pairs={{0,16},{16,0},{1,17},{17,1},{2,18},{18,2},{3,19},{19,3},{4,20},{20... | collective-permute-start | bytes 6291464 | tf_op jit(solution)/shard_map/ppermute | solution.py:17
  914.3 16.6 %copy-start.14 = (bf16[2048,512]{1,0:T(8,128)(2,1)S(1)}, bf16[2048,512]{1,0:T(8,128)(2,1)}, u32[]{:S(2)}) copy-start(bf16[2048,512]{1,0:T(8,128)(2,1)} %copy-done.13) | copy-start | bytes 6291460
Sparse Core Ops, SparseCore 0:
  23.1 79.4 reduce-scatter.4
  105.0 77.2 reduce-scatter.6
  185.2 77.2 reduce-scatter.8
  265.3 77.2 reduce-scatter.10
  344.5 132.7 all-gather.8
  479.2 128.5 all-gather.4
  609.9 128.5 all-gather.6
  740.5 128.5 all-gather.10

commit v2 on v1

--- a/solution.py
+++ b/solution.py
@@ -1,8 +1,11 @@
+import functools
 import math
 
 import jax
 import jax.numpy as jnp
 from jax import lax
+from jax.experimental import pallas as pl
+from jax.experimental.pallas import tpu as pltpu
 from jax.sharding import PartitionSpec as P
 
 M = 8192
@@ -16,6 +19,71 @@
         return lax.psum(block.astype(jnp.bfloat16), "row").astype(jnp.float32)
     moved = lax.ppermute(block.astype(jnp.bfloat16), "row", [(0, 1), (1, 0)])
     return block.astype(jnp.float32) + moved.astype(jnp.float32)
+
+
+def after(value, earlier):
+    return lax.optimization_barrier((value, earlier))[0]
+
+
+def gather_pairs(block):
+    middle = (lax.axis_index("depth") == 1) | (lax.axis_index("depth") == 2)
+    outer = lax.ppermute(block, "depth", [(0, 1), (1, 0), (2, 3), (3, 2)])
+    inner = lax.ppermute(block, "depth", [(1, 2), (2, 1)])
+    far_inner = lax.ppermute(outer, "depth", [(1, 2), (2, 1)])
+    far_outer = lax.ppermute(inner, "depth", [(2, 3), (1, 0)])
+    last = lax.ppermute(far_inner, "depth", [(2, 3), (1, 0)])
+    near = jnp.concatenate([block, outer], axis=1)
+    far = jnp.concatenate(
+        [jnp.where(middle, inner, far_outer), jnp.where(middle, far_inner, last)], axis=1
+    )
+    held = []
+    for pair in (near, far):
+        other = lax.ppermute(pair, "col", [(0, 2), (1, 3), (2, 0), (3, 1)])
+        held += [pair, other]
+    return (far, held[1]), held + [lax.ppermute(pair, "col", [(0, 1), (1, 0), (2, 3), (3, 2)]) for pair in held]
+
+
+def gather(block):
+    sizes = (lax.axis_size("row"), lax.axis_size("col"), lax.axis_size("depth"))
+    if sizes == (2, 4, 4):
+        return gather_pairs(block)
+    return block, [lax.all_gather(block, ("col", "depth"), axis=1, tiled=True)]
+
+
+def product_tile(summed, *refs):
+    *parts, gram, out = refs[1:] if summed else refs
+    width = parts[0].shape[1]
+    total = refs[0][...] if summed else None
+    for i, part in enumerate(parts):
+        term = jnp.dot(
+            part[...], gram[i * width : (i + 1) * width, :], preferred_element_type=jnp.float32
+        )
+        total = term if total is None else total + term
+    out[...] = total
+
+
+def add_product(running, parts, gram):
+    rows, width = parts[0].shape
+    columns = gram.shape[1]
+    tile = min(rows, 256)
+    summed = running is not None
+    wide = pl.BlockSpec((tile, columns), lambda i: (i, 0))
+    return pl.pallas_call(
+        functools.partial(product_tile, summed),
+        grid=(rows // tile,),
+        out_shape=jax.ShapeDtypeStruct((rows, columns), jnp.float32),
+        in_specs=[wide] * summed
+        + [pl.BlockSpec((tile, width), lambda i: (i, 0))] * len(parts)
+        + [pl.BlockSpec(gram.shape, lambda i: (0, 0))],
+        out_specs=wide,
+        input_output_aliases={0: 0} if summed else {},
+        compiler_params=pltpu.CompilerParams(vmem_limit_bytes=32 * 2**20),
+        cost_estimate=pl.CostEstimate(
+            flops=2 * rows * gram.shape[0] * columns,
+            bytes_accessed=2 * rows * gram.shape[0] + 8 * rows * columns,
+            transcendentals=0,
+        ),
+    )(*([running] if summed else []), *parts, gram)
 
 
 def body(grad_partial, grad_scale, momentum):
@@ -38,34 +106,44 @@
         scaled = lax.optimization_barrier(scaled)
         sums.append(lax.psum_scatter(scaled, "depth", scatter_dimension=0))
 
-    momenta, mine, squares = [], [], []
+    momenta, mine, squares, panels = [], [], [], []
+    relayed = None
     for j in range(PIECES):
         gradient = sums[j]
-        if mine:
-            gradient, mine[-1] = lax.optimization_barrier((gradient, mine[-1]))
+        if relayed is not None:
+            gradient = after(gradient, relayed)
         gradient = gradient.astype(jnp.float32)
         new = BETA * lax.slice_in_dim(momentum, j * width, (j + 1) * width, axis=1) + gradient
         nesterov = gradient + BETA * new
-        new, kept, square = lax.optimization_barrier(
-            (new, nesterov.astype(jnp.bfloat16), jnp.sum(nesterov * nesterov))
+        kept, square = lax.optimization_barrier(
+            (nesterov.astype(jnp.bfloat16), jnp.sum(nesterov * nesterov))
         )
         momenta.append(new)
         mine.append(kept)
         squares.append(square)
+        relayed, held = gather(kept)
+        if panels:
+            relayed = (relayed, panels[-1])
+        panels.append(held)
     total_sq = lax.psum(sum(squares), ("row", "col", "depth"))
     factor = math.sqrt(M) / (1.5 * (jnp.sqrt(total_sq) + EPSILON))
     own = jnp.concatenate(mine, axis=1)
 
     product = None
     for j in range(PIECES):
-        panel = lax.all_gather(mine[j], ("col", "depth"), axis=1, tiled=True)
-        gram = lax.dot_general(
-            panel, own, (((0,), (0,)), ((), ())), preferred_element_type=jnp.float32
+        held = panels[j]
+        gram = jnp.concatenate(
+            [
+                lax.dot_general(
+                    part, own, (((0,), (0,)), ((), ())), preferred_element_type=jnp.float32
+                ).astype(jnp.bfloat16)
+                for part in held
+            ],
+            axis=0,
         )
-        gram = row_sum(gram.astype(jnp.bfloat16))
+        gram = row_sum(gram)
         gram = (gram * (factor * factor)).astype(jnp.bfloat16)
-        term = jnp.dot(panel, gram, preferred_element_type=jnp.float32)
-        product = term if product is None else product + term
+        product = add_product(product, held, gram)
     update = (math.sqrt(M) * factor) * (1.5 * own.astype(jnp.float32) - 0.5 * product)
     return (jnp.concatenate(momenta, axis=1), update)
 

time: 969 us -> 974 us (level)
  waiting for transfers between devices: 706 us -> 587 us
  Pallas kernels: 0 us -> 75.8 us
  starting transfers between devices: 6.33 us -> 48.3 us
  matrix products: 128 us -> 97.3 us
  other arithmetic: 49 us -> 74.7 us
    ppermute x0 -> x44, waiting for transfers between devices: none -> 462 us  [the longest x4 167 us: gather_pairs(): last = lax.ppermute(far_inner, 'depth', [(2, 3), (1, 0)])]
    all_gather x4 -> x0, waiting for transfers between devices: 413 us -> none  [body(): panel = lax.all_gather(mine[j], ('col', 'depth'), axis=1, tiled=True)]
    reduce_scatter x4, waiting for transfers between devices: 291 us -> 71 us  [body(): sums.append(lax.psum_scatter(scaled, 'depth', scatter_dimension=0))]
    pallas_call x0 -> x4, Pallas kernels: none -> 75.8 us  [add_product(): pl.pallas_call(functools.partial(product_tile, summed), grid=(rows // til...]
    ppermute x4, waiting for transfers between devices: 0.79 us -> 53.7 us  [row_sum(): moved = lax.ppermute(block.astype(jnp.bfloat16), 'row', [(0, 1), (1, 0)])]
    ppermute x0 -> x44, starting transfers between devices: none -> 43.9 us  [the longest x8 12.4 us: gather_pairs(): other = lax.ppermute(pair, 'col', [(0, 2), (1, 3), (2, 0), (3, 1)])]
    dot_general x8 -> x32, matrix products: 128 us -> 97.3 us  [body(): lax.dot_general(part, own, (((0,), (0,)), ((), ())), preferred_element_ty...]
    reduce_sum x4 -> x1, other arithmetic: 19.3 us -> 3.21 us  [body(): jnp.sum(nesterov * nesterov)]
  transfers between devices with their start and end apart: 12 -> 52, of which waited for: 9 -> 19; matrix products, arithmetic and copies ran while one was open for 15% -> 16% of each run, Pallas kernels for 0% -> 6%
where the time goes in v2:
time: 974 us; the launch traced here: 964 us
  waiting for transfers between devices  587 us (60%)
  matrix products  97.3 us (10%)
  Pallas kernels  75.8 us (8%)
  other arithmetic  74.7 us (8%)
  starting transfers between devices  48.3 us (5%)
  blocking collectives  44.3 us (5%)
  local copies, waits for them, and re-layouts  18.5 us (2%)
  between operations  17.9 us (2%)
    ppermute x4, waiting for transfers between devices, gather_pairs(): last = lax.ppermute(far_inner, 'depth', [(2, 3), (1, 0)])  167 us
    ppermute x4, waiting for transfers between devices, gather_pairs(): outer = lax.ppermute(block, 'depth', [(0, 1), (1, 0), (2, 3), (3, 2)])  118 us
    ppermute x8, waiting for transfers between devices, gather_pairs(): other = lax.ppermute(pair, 'col', [(0, 2), (1, 3), (2, 0), (3, 1)])  111 us
    dot_general x32, matrix products, body(): lax.dot_general(part, own, (((0,), (0,)), ((), ())), preferred_element_ty...  97.3 us
    pallas_call x4, Pallas kernels, add_product(): pl.pallas_call(functools.partial(product_tile, summed), grid=(rows // til...  75.8 us
    reduce_scatter x4, waiting for transfers between devices, body(): sums.append(lax.psum_scatter(scaled, 'depth', scatter_dimension=0))  71 us
    ppermute x4, waiting for transfers between devices, gather_pairs(): far_outer = lax.ppermute(inner, 'depth', [(2, 3), (1, 0)])  65.6 us
    ppermute x4, waiting for transfers between devices, row_sum(): moved = lax.ppermute(block.astype(jnp.bfloat16), 'row', [(0, 1), (1, 0)])  53.7 us
  transfers between devices with their start and end apart: 52, of which 19 were waited for; matrix products, arithmetic and copies ran while one was open for 16% of the time, Pallas kernels for 6%

profile of v2, /device:TPU:0, one launch (start us, length us, event | category | flops | bytes accessed | tf_op | source)
XLA Modules:
  0.0 963.9 jit_solution(6309631922944483550)
XLA Ops:
  8.1 4.8 fusion.14
  13.0 7.7 fusion.15
  31.6 71.0 %reduce-scatter.5.cloned.1.call-done = bf16[1,4096,128]{2,1,0:T(8,128)(2,1)} async-done(((bf16[4,4096,128]{2,1,0:T(8,128)(2,1)}), bf16[1,4096,128]{2,1,0:T(8,128)(2,1)}) %reduce-scatter.5.cloned.1.call-update) | async-done | bytes 1048592 | tf_op jit(solution)/shard_map/reduce_scatter | solution.py:107
  102.6 4.3 convert_add_fusion.1
  109.1 58.4 %collective-permute-done.2 = bf16[4096,128]{1,0:T(8,128)(2,1)} collective-permute-done((bf16[4096,128]{1,0:T(8,128)(2,1)S(1)}, bf16[4096,128]{1,0:T(8,128)(2,1)}, u32[]{:S(2)}, u32[]{:S(2)}) %collective-permute-start.2) | collective-permute-done | bytes 1048608 | tf_op jit(solution)/shard_map/ppermute | solution.py:30
  176.2 45.7 %collective-permute-done.1 = bf16[4096,128]{1,0:T(8,128)(2,1)} collective-permute-done((bf16[4096,128]{1,0:T(8,128)(2,1)S(1)}, bf16[4096,128]{1,0:T(8,128)(2,1)}, u32[]{:S(2)}, u32[]{:S(2)}) %collective-permute-start.1) | collective-permute-done | bytes 1048608 | tf_op jit(solution)/shard_map/ppermute | solution.py:33
  223.2 82.4 %collective-permute-done.4 = bf16[4096,128]{1,0:T(8,128)(2,1)S(1)} collective-permute-done((bf16[4096,128]{1,0:T(8,128)(2,1)S(1)}, bf16[4096,128]{1,0:T(8,128)(2,1)S(1)}, u32[]{:S(2)}, u32[]{:S(2)}) %collective-permute-start.4) | collective-permute-done | bytes 1048608 | tf_op jit(solution)/shard_map/ppermute | solution.py:34
  308.4 4.6 convert_add_fusion.7
  313.7 25.1 %collective-permute-done.8 = bf16[4096,128]{1,0:T(8,128)(2,1)S(1)} collective-permute-done((bf16[4096,128]{1,0:T(8,128)(2,1)S(1)}, bf16[4096,128]{1,0:T(8,128)(2,1)S(1)}, u32[]{:S(2)}, u32[]{:S(2)}) %collective-permute-start.8) | collective-permute-done | bytes 1048608 | tf_op jit(solution)/shard_map/ppermute | solution.py:30
  349.5 36.6 %collective-permute-done.12.refs_3_ = bf16[4096,256]{1,0:T(8,128)(2,1)} collective-permute-done((bf16[4096,256]{1,0:T(8,128)(2,1)}, bf16[4096,256]{1,0:T(8,128)(2,1)}, u32[]{:S(2)}, u32[]{:S(2)}) %collective-permute-start.12) | collective-permute-done | bytes 2097184 | tf_op jit(solution)/shard_map/ppermute | solution.py:41
  387.9 42.8 %collective-permute-done.10 = bf16[4096,128]{1,0:T(8,128)(2,1)} collective-permute-done((bf16[4096,128]{1,0:T(8,128)(2,1)S(1)}, bf16[4096,128]{1,0:T(8,128)(2,1)}, u32[]{:S(2)}, u32[]{:S(2)}) %collective-permute-start.10) | collective-permute-done | bytes 1048608 | tf_op jit(solution)/shard_map/ppermute | solution.py:34
  435.2 4.5 convert_add_fusion.5
  444.1 34.9 %collective-permute-done.19 = bf16[4096,128]{1,0:T(8,128)(2,1)S(1)} collective-permute-done((bf16[4096,128]{1,0:T(8,128)(2,1)S(1)}, bf16[4096,128]{1,0:T(8,128)(2,1)S(1)}, u32[]{:S(2)}, u32[]{:S(2)}) %collective-permute-start.19) | collective-permute-done | bytes 1048608 | tf_op jit(solution)/shard_map/ppermute | solution.py:30
  489.0 19.9 %collective-permute-done.18 = bf16[4096,128]{1,0:T(8,128)(2,1)} collective-permute-done((bf16[4096,128]{1,0:T(8,128)(2,1)}, bf16[4096,128]{1,0:T(8,128)(2,1)}, u32[]{:S(2)}, u32[]{:S(2)}) %collective-permute-start.18) | collective-permute-done | bytes 1048608 | tf_op jit(solution)/shard_map/ppermute | solution.py:33
  509.3 21.3 %collective-permute-done.21 = bf16[4096,128]{1,0:T(8,128)(2,1)} collective-permute-done((bf16[4096,128]{1,0:T(8,128)(2,1)}, bf16[4096,128]{1,0:T(8,128)(2,1)}, u32[]{:S(2)}, u32[]{:S(2)}) %collective-permute-start.21) | collective-permute-done | bytes 1048608 | tf_op jit(solution)/shard_map/ppermute | solution.py:34
  535.8 19.4 %collective-permute-done.22.refs_2_ = bf16[4096,256]{1,0:T(8,128)(2,1)} collective-permute-done((bf16[4096,256]{1,0:T(8,128)(2,1)}, bf16[4096,256]{1,0:T(8,128)(2,1)}, u32[]{:S(2)}, u32[]{:S(2)}) %collective-permute-start.22) | collective-permute-done | bytes 2097184 | tf_op jit(solution)/shard_map/ppermute | solution.py:41
  559.6 5.1 fusion.51
  571.8 6.7 collective-permute-start.36
  633.3 4.9 fusion.34
  640.2 44.3 %psum.7 = f32[]{:T(128)} all-reduce(f32[]{:T(128)S(6)} %add.68), channel_id=1, replica_groups=mesh['row'=2,'col'=4,'depth'=4] {'row','col','depth'}, use_global_device_ids=true, to_apply=%region_8.9 | all-reduce | flops 1 | bytes 8 | tf_op jit(solution)/shard_map/psum | solution.py:128
  690.2 4.8 fusion.27
  699.9 19.5 %shard_map.50.refs_0_ = f32[4096,512]{1,0:T(8,128)} custom-call(bf16[4096,256]{1,0:T(8,128)(2,1)} %constant_dynamic-update-slice_fusion.refs_0_, bf16[4096,256]{1,0:T(8,128)(2,1)} %collective-permute-done.5.refs_1_, bf16[4096,256]{1,0:T(8,128)(2,1)} %pad_maximum_fusion.5.refs_2_, bf16[4096,256]{1,0:T(8,128)(2,1)} %collective-permute-done.12.refs_3_, ...), custom_call_target="tpu_custom_call" | custom-call | flops 8589934592 | bytes 33554432 | tf_op jit(solution)/shard_map/pallas_call | solution.py:71
  719.4 12.9 %collective-permute-done.30.refs_4_ = bf16[4096,256]{1,0:T(8,128)(2,1)S(1)} collective-permute-done((bf16[4096,256]{1,0:T(8,128)(2,1)}, bf16[4096,256]{1,0:T(8,128)(2,1)S(1)}, u32[]{:S(2)}, u32[]{:S(2)}) %collective-permute-start.30) | collective-permute-done | bytes 2097184 | tf_op jit(solution)/shard_map/ppermute | solution.py:41
  742.3 20.4 %collective-permute-done.41 = bf16[4096,128]{1,0:T(8,128)(2,1)S(1)} collective-permute-done((bf16[4096,128]{1,0:T(8,128)(2,1)S(1)}, bf16[4096,128]{1,0:T(8,128)(2,1)S(1)}, u32[]{:S(2)}, u32[]{:S(2)}) %collective-permute-start.41) | collective-permute-done | bytes 1048608 | tf_op jit(solution)/shard_map/ppermute | solution.py:34
  768.3 14.2 %collective-permute-done.29 = bf16[2048,512]{1,0:T(8,128)(2,1)S(1)} collective-permute-done((bf16[2048,512]{1,0:T(8,128)(2,1)}, bf16[2048,512]{1,0:T(8,128)(2,1)S(1)}, u32[]{:S(2)}, u32[]{:S(2)}) %collective-permute-start.29) | collective-permute-done | bytes 2097184 | tf_op jit(solution)/shard_map/ppermute | solution.py:20
  793.5 39.8 %collective-permute-done.42.refs_4_ = bf16[4096,256]{1,0:T(8,128)(2,1)S(1)} collective-permute-done((bf16[4096,256]{1,0:T(8,128)(2,1)S(1)}, bf16[4096,256]{1,0:T(8,128)(2,1)S(1)}, u32[]{:S(2)}, u32[]{:S(2)}) %collective-permute-start.42) | collective-permute-done | bytes 2097184 | tf_op jit(solution)/shard_map/ppermute | solution.py:41
  847.2 20.1 %shard_map.51.refs_0_ = f32[4096,512]{1,0:T(8,128)} custom-call(f32[4096,512]{1,0:T(8,128)} %shard_map.50.refs_0_, bf16[4096,256]{1,0:T(8,128)(2,1)} %constant_dynamic-update-slice_fusion.2.refs_1_, bf16[4096,256]{1,0:T(8,128)(2,1)} %collective-permute-done.11.refs_2_, ...), custom_call_target="tpu_custom_call", output_to_operand_aliasing={{}: (0, {})} | custom-call | flops 8589934592 | bytes 33554432 | tf_op jit(solution)/shard_map/pallas_call | solution.py:71
  867.3 16.7 %collective-permute-done.35 = bf16[2048,512]{1,0:T(8,128)(2,1)} collective-permute-done((bf16[2048,512]{1,0:T(8,128)(2,1)}, bf16[2048,512]{1,0:T(8,128)(2,1)}, u32[]{:S(2)}, u32[]{:S(2)}) %collective-permute-start.35) | collective-permute-done | bytes 2097184 | tf_op jit(solution)/shard_map/ppermute | solution.py:20
  886.9 18.8 %shard_map.52.refs_0_ = f32[4096,512]{1,0:T(8,128)} custom-call(f32[4096,512]{1,0:T(8,128)} %shard_map.51.refs_0_, bf16[4096,256]{1,0:T(8,128)(2,1)} %constant_dynamic-update-slice_fusion.4.refs_1_, bf16[4096,256]{1,0:T(8,128)(2,1)} %collective-permute-done.22.refs_2_, bf16[4096,256]{1,0:T(8,128)(2,1)S(1)} %copy-done, ...), custom_call_target="tpu_custom_call", output_to_operand_aliasing={{}: (0, {})} | custom-call | flops 8589934592 | bytes 33554432 | tf_op jit(solution)/shard_map/pallas_call | solution.py:71
  905.8 22.8 %collective-permute-done.47 = bf16[2048,512]{1,0:T(8,128)(2,1)} collective-permute-done((bf16[2048,512]{1,0:T(8,128)(2,1)}, bf16[2048,512]{1,0:T(8,128)(2,1)}, u32[]{:S(2)}, u32[]{:S(2)}) %collective-permute-start.47) | collective-permute-done | bytes 2097184 | tf_op jit(solution)/shard_map/ppermute | solution.py:20
  931.5 17.4 %shard_map.53 = f32[4096,512]{1,0:T(8,128)} custom-call(f32[4096,512]{1,0:T(8,128)} %shard_map.52.refs_0_, bf16[4096,256]{1,0:T(8,128)(2,1)S(1)} %copy-done.1, bf16[4096,256]{1,0:T(8,128)(2,1)S(1)} %collective-permute-done.37.refs_2_, bf16[4096,256]{1,0:T(8,128)(2,1)S(1)} %pad_maximum_fusion.8.refs_3_, ...), custom_call_target="tpu_custom_call", output_to_operand_aliasing={{}: (0, {})} | custom-call | flops 8589934592 | bytes 33554432 | tf_op jit(solution)/shard_map/pallas_call | solution.py:71
  948.8 8.3 subtract_multiply_fusion
  (240 shorter events, 185.8 us)
Async XLA Ops:
  7.2 95.5 %reduce-scatter.5.cloned.1.call-start = ((), (), s32[]{:S(2)}) async-start(), calls=%async_computation.4 | async-start | bytes 5242880 | tf_op jit(solution)/shard_map/reduce_scatter | solution.py:107
  23.0 285.3 %reduce-scatter.7.cloned.1.call-start = ((), (), s32[]{:S(2)}) async-start(), calls=%async_computation.5 | async-start | bytes 5242880 | tf_op jit(solution)/shard_map/reduce_scatter | solution.py:107
  26.4 408.6 %reduce-scatter.9.cloned.1.call-start = ((), (), s32[]{:S(2)}) async-start(), calls=%async_computation.6 | async-start | bytes 5242880 | tf_op jit(solution)/shard_map/reduce_scatter | solution.py:107
  31.6 523.6 %reduce-scatter.11.cloned.1.call-start = ((), (), s32[]{:S(2)}) async-start(), calls=%async_computation.7 | async-start | bytes 5242880 | tf_op jit(solution)/shard_map/reduce_scatter | solution.py:107
  106.9 60.6 %collective-permute-start.2 = (bf16[4096,128]{1,0:T(8,128)(2,1)S(1)}, bf16[4096,128]{1,0:T(8,128)(2,1)}, u32[]{:S(2)}, u32[]{:S(2)}) collective-permute-start(bf16[4096,128]{1,0:T(8,128)(2,1)S(1)} %get-tuple-element.13), channel_id=1, source_target_pairs={{0,1},{1,0},{2,3},{3,2},{4,5},{5,4},{6,7},{7,6},{8,9},{9,8},{10,11... | collective-permute-start | bytes 3145736 | tf_op jit(solution)/shard_map/ppermute | solution.py:30
  108.4 59.9 %collective-permute-start = (bf16[4096,128]{1,0:T(8,128)(2,1)S(1)}, bf16[4096,128]{1,0:T(8,128)(2,1)S(1)}, u32[]{:S(2)}, u32[]{:S(2)}) collective-permute-start(bf16[4096,128]{1,0:T(8,128)(2,1)S(1)} %get-tuple-element.13), channel_id=1, source_target_pairs={{1,2},{2,1},{5,6},{6,5},{9,10},{10,9},{13,14},{14,13},{17,18},{18,... | collective-permute-start | bytes 3145736 | tf_op jit(solution)/shard_map/ppermute | solution.py:31
  168.3 53.6 %collective-permute-start.1 = (bf16[4096,128]{1,0:T(8,128)(2,1)S(1)}, bf16[4096,128]{1,0:T(8,128)(2,1)}, u32[]{:S(2)}, u32[]{:S(2)}) collective-permute-start(bf16[4096,128]{1,0:T(8,128)(2,1)S(1)} %collective-permute-done), channel_id=1, source_target_pairs={{2,3},{1,0},{6,7},{5,4},{10,11},{9,8},{14,15},{13,12},{18,19},{17,... | collective-permute-start | bytes 3145736 | tf_op jit(solution)/shard_map/ppermute | solution.py:33
  171.2 134.4 %collective-permute-start.4 = (bf16[4096,128]{1,0:T(8,128)(2,1)S(1)}, bf16[4096,128]{1,0:T(8,128)(2,1)S(1)}, u32[]{:S(2)}, u32[]{:S(2)}) collective-permute-start(bf16[4096,128]{1,0:T(8,128)(2,1)S(1)} %collective-permute-done.3), channel_id=1, source_target_pairs={{2,3},{1,0},{6,7},{5,4},{10,11},{9,8},{14,15},{13,12},{18,19},{17,... | collective-permute-start | bytes 3145736 | tf_op jit(solution)/shard_map/ppermute | solution.py:34
  174.8 133.6 %collective-permute-start.5 = (bf16[4096,256]{1,0:T(8,128)(2,1)}, bf16[4096,256]{1,0:T(8,128)(2,1)}, u32[]{:S(2)}, u32[]{:S(2)}) collective-permute-start(bf16[4096,256]{1,0:T(8,128)(2,1)} %constant_dynamic-update-slice_fusion.refs_0_), channel_id=1, source_target_pairs={{0,8},{4,12},{8,0},{12,4},{1,9},{5,13},{9,1},{13,5},{2,10},{6,14},... | collective-permute-start | bytes 6291464 | tf_op jit(solution)/shard_map/ppermute | solution.py:41
  342.5 88.2 %collective-permute-start.10 = (bf16[4096,128]{1,0:T(8,128)(2,1)S(1)}, bf16[4096,128]{1,0:T(8,128)(2,1)}, u32[]{:S(2)}, u32[]{:S(2)}) collective-permute-start(bf16[4096,128]{1,0:T(8,128)(2,1)S(1)} %collective-permute-done.9), channel_id=1, source_target_pairs={{2,3},{1,0},{6,7},{5,4},{10,11},{9,8},{14,15},{13,12},{18,19},{17,... | collective-permute-start | bytes 3145736 | tf_op jit(solution)/shard_map/ppermute | solution.py:34
  346.2 88.9 %collective-permute-start.13 = (bf16[4096,256]{1,0:T(8,128)(2,1)}, bf16[4096,256]{1,0:T(8,128)(2,1)}, u32[]{:S(2)}, u32[]{:S(2)}) collective-permute-start(bf16[4096,256]{1,0:T(8,128)(2,1)} %constant_dynamic-update-slice_fusion.refs_0_), channel_id=1, source_target_pairs={{0,4},{4,0},{8,12},{12,8},{1,5},{5,1},{9,13},{13,9},{2,6},{6,2},{1... | collective-permute-start | bytes 6291464 | tf_op jit(solution)/shard_map/ppermute | solution.py:43
  346.3 88.8 %collective-permute-start.15 = (bf16[4096,256]{1,0:T(8,128)(2,1)}, bf16[4096,256]{1,0:T(8,128)(2,1)}, u32[]{:S(2)}, u32[]{:S(2)}) collective-permute-start(bf16[4096,256]{1,0:T(8,128)(2,1)} %pad_maximum_fusion.5.refs_2_), channel_id=1, source_target_pairs={{0,4},{4,0},{8,12},{12,8},{1,5},{5,1},{9,13},{13,9},{2,6},{6,2},{1... | collective-permute-start | bytes 6291464 | tf_op jit(solution)/shard_map/ppermute | solution.py:43
  386.1 48.9 %collective-permute-start.14 = (bf16[4096,256]{1,0:T(8,128)(2,1)}, bf16[4096,256]{1,0:T(8,128)(2,1)}, u32[]{:S(2)}, u32[]{:S(2)}) collective-permute-start(bf16[4096,256]{1,0:T(8,128)(2,1)} %collective-permute-done.5.refs_1_), channel_id=1, source_target_pairs={{0,4},{4,0},{8,12},{12,8},{1,5},{5,1},{9,13},{13,9},{2,6},{6,2},{1... | collective-permute-start | bytes 6291464 | tf_op jit(solution)/shard_map/ppermute | solution.py:43
  386.2 48.9 %collective-permute-start.11 = (bf16[4096,256]{1,0:T(8,128)(2,1)}, bf16[4096,256]{1,0:T(8,128)(2,1)}, u32[]{:S(2)}, u32[]{:S(2)}) collective-permute-start(bf16[4096,256]{1,0:T(8,128)(2,1)} %constant_dynamic-update-slice_fusion.2.refs_1_), channel_id=1, source_target_pairs={{0,8},{4,12},{8,0},{12,4},{1,9},{5,13},{9,1},{13,5},{2,10},{6,14},... | collective-permute-start | bytes 6291464 | tf_op jit(solution)/shard_map/ppermute | solution.py:41
  482.0 48.5 %collective-permute-start.21 = (bf16[4096,128]{1,0:T(8,128)(2,1)}, bf16[4096,128]{1,0:T(8,128)(2,1)}, u32[]{:S(2)}, u32[]{:S(2)}) collective-permute-start(bf16[4096,128]{1,0:T(8,128)(2,1)} %collective-permute-done.20), channel_id=1, source_target_pairs={{2,3},{1,0},{6,7},{5,4},{10,11},{9,8},{14,15},{13,12},{18,19},{17,... | collective-permute-start | bytes 3145736 | tf_op jit(solution)/shard_map/ppermute | solution.py:34
  485.0 50.3 %collective-permute-start.24 = (bf16[4096,256]{1,0:T(8,128)(2,1)}, bf16[4096,256]{1,0:T(8,128)(2,1)}, u32[]{:S(2)}, u32[]{:S(2)}) collective-permute-start(bf16[4096,256]{1,0:T(8,128)(2,1)} %constant_dynamic-update-slice_fusion.2.refs_1_), channel_id=1, source_target_pairs={{0,4},{4,0},{8,12},{12,8},{1,5},{5,1},{9,13},{13,9},{2,6},{6,2},{1... | collective-permute-start | bytes 6291464 | tf_op jit(solution)/shard_map/ppermute | solution.py:43
  485.1 70.1 %collective-permute-start.25 = (bf16[4096,256]{1,0:T(8,128)(2,1)}, bf16[4096,256]{1,0:T(8,128)(2,1)}, u32[]{:S(2)}, u32[]{:S(2)}) collective-permute-start(bf16[4096,256]{1,0:T(8,128)(2,1)} %collective-permute-done.11.refs_2_), channel_id=1, source_target_pairs={{0,4},{4,0},{8,12},{12,8},{1,5},{5,1},{9,13},{13,9},{2,6},{6,2},{1... | collective-permute-start | bytes 6291464 | tf_op jit(solution)/shard_map/ppermute | solution.py:43
  488.9 66.3 %collective-permute-start.26 = (bf16[4096,256]{1,0:T(8,128)(2,1)S(1)}, bf16[4096,256]{1,0:T(8,128)(2,1)}, u32[]{:S(2)}, u32[]{:S(2)}) collective-permute-start(bf16[4096,256]{1,0:T(8,128)(2,1)S(1)} %pad_maximum_fusion.6.refs_3_), channel_id=1, source_target_pairs={{0,4},{4,0},{8,12},{12,8},{1,5},{5,1},{9,13},{13,9},{2,6},{6,2},{1... | collective-permute-start | bytes 6291464 | tf_op jit(solution)/shard_map/ppermute | solution.py:43
  535.3 199.0 %collective-permute-start.31 = (bf16[4096,256]{1,0:T(8,128)(2,1)}, bf16[4096,256]{1,0:T(8,128)(2,1)}, u32[]{:S(2)}, u32[]{:S(2)}) collective-permute-start(bf16[4096,256]{1,0:T(8,128)(2,1)} %constant_dynamic-update-slice_fusion.4.refs_1_), channel_id=1, source_target_pairs={{0,4},{4,0},{8,12},{12,8},{1,5},{5,1},{9,13},{13,9},{2,6},{6,2},{1... | collective-permute-start | bytes 6291464 | tf_op jit(solution)/shard_map/ppermute | solution.py:43
  555.2 207.8 %collective-permute-start.32 = (bf16[4096,256]{1,0:T(8,128)(2,1)}, bf16[4096,256]{1,0:T(8,128)(2,1)}, u32[]{:S(2)}, u32[]{:S(2)}) collective-permute-start(bf16[4096,256]{1,0:T(8,128)(2,1)} %collective-permute-done.22.refs_2_), channel_id=1, source_target_pairs={{0,4},{4,0},{8,12},{12,8},{1,5},{5,1},{9,13},{13,9},{2,6},{6,2},{1... | collective-permute-start | bytes 6291464 | tf_op jit(solution)/shard_map/ppermute | solution.py:43
  571.8 113.4 %collective-permute-start.36 = (bf16[4096,128]{1,0:T(8,128)(2,1)S(1)}, bf16[4096,128]{1,0:T(8,128)(2,1)}, u32[]{:S(2)}, u32[]{:S(2)}) collective-permute-start(bf16[4096,128]{1,0:T(8,128)(2,1)S(1)} %get-tuple-element.23), channel_id=1, source_target_pairs={{0,1},{1,0},{2,3},{3,2},{4,5},{5,4},{6,7},{7,6},{8,9},{9,8},{10,11... | collective-permute-start | bytes 3145736 | tf_op jit(solution)/shard_map/ppermute | solution.py:30
  578.5 116.5 %collective-permute-start.38 = (bf16[4096,128]{1,0:T(8,128)(2,1)S(1)}, bf16[4096,128]{1,0:T(8,128)(2,1)}, u32[]{:S(2)}, u32[]{:S(2)}) collective-permute-start(bf16[4096,128]{1,0:T(8,128)(2,1)S(1)} %get-tuple-element.23), channel_id=1, source_target_pairs={{1,2},{2,1},{5,6},{6,5},{9,10},{10,9},{13,14},{14,13},{17,18},{18,... | collective-permute-start | bytes 3145736 | tf_op jit(solution)/shard_map/ppermute | solution.py:31
  603.5 92.2 %collective-permute-start.28 = (bf16[2048,512]{1,0:T(8,128)(2,1)}, bf16[2048,512]{1,0:T(8,128)(2,1)}, u32[]{:S(2)}, u32[]{:S(2)}) collective-permute-start(bf16[2048,512]{1,0:T(8,128)(2,1)} %fusion.44), channel_id=1, source_target_pairs={{0,16},{16,0},{1,17},{17,1},{2,18},{18,2},{3,19},{19,3},{4,20},{20... | collective-permute-start | bytes 6291464 | tf_op jit(solution)/shard_map/ppermute | solution.py:20
  732.3 52.5 %collective-permute-start.33 = (bf16[4096,256]{1,0:T(8,128)(2,1)S(1)}, bf16[4096,256]{1,0:T(8,128)(2,1)S(1)}, u32[]{:S(2)}, u32[]{:S(2)}) collective-permute-start(bf16[4096,256]{1,0:T(8,128)(2,1)S(1)} %copy-done), channel_id=1, source_target_pairs={{0,4},{4,0},{8,12},{12,8},{1,5},{5,1},{9,13},{13,9},{2,6},{6,2},{1... | collective-permute-start | bytes 6291464 | tf_op jit(solution)/shard_map/ppermute | solution.py:43
  740.6 48.5 %collective-permute-start.37 = (bf16[4096,256]{1,0:T(8,128)(2,1)S(1)}, bf16[4096,256]{1,0:T(8,128)(2,1)S(1)}, u32[]{:S(2)}, u32[]{:S(2)}) collective-permute-start(bf16[4096,256]{1,0:T(8,128)(2,1)S(1)} %copy-done.1), channel_id=1, source_target_pairs={{0,8},{4,12},{8,0},{12,4},{1,9},{5,13},{9,1},{13,5},{2,10},{6,14},... | collective-permute-start | bytes 6291464 | tf_op jit(solution)/shard_map/ppermute | solution.py:41
  762.7 70.6 %collective-permute-start.34 = (bf16[4096,256]{1,0:T(8,128)(2,1)S(1)}, bf16[4096,256]{1,0:T(8,128)(2,1)S(1)}, u32[]{:S(2)}, u32[]{:S(2)}) collective-permute-start(bf16[4096,256]{1,0:T(8,128)(2,1)S(1)} %collective-permute-done.30.refs_4_), channel_id=1, source_target_pairs={{0,4},{4,0},{8,12},{12,8},{1,5},{5,1},{9,13},{13,9},{2,6},{6,2},{1... | collective-permute-start | bytes 6291464 | tf_op jit(solution)/shard_map/ppermute | solution.py:43
  763.0 70.2 %collective-permute-start.42 = (bf16[4096,256]{1,0:T(8,128)(2,1)S(1)}, bf16[4096,256]{1,0:T(8,128)(2,1)S(1)}, u32[]{:S(2)}, u32[]{:S(2)}) collective-permute-start(bf16[4096,256]{1,0:T(8,128)(2,1)S(1)} %pad_maximum_fusion.8.refs_3_), channel_id=1, source_target_pairs={{0,8},{4,12},{8,0},{12,4},{1,9},{5,13},{9,1},{13,5},{2,10},{6,14},... | collective-permute-start | bytes 6291464 | tf_op jit(solution)/shard_map/ppermute | solution.py:41
  782.5 55.7 %collective-permute-start.43 = (bf16[4096,256]{1,0:T(8,128)(2,1)S(1)}, bf16[4096,256]{1,0:T(8,128)(2,1)S(1)}, u32[]{:S(2)}, u32[]{:S(2)}) collective-permute-start(bf16[4096,256]{1,0:T(8,128)(2,1)S(1)} %copy-done.1), channel_id=1, source_target_pairs={{0,4},{4,0},{8,12},{12,8},{1,5},{5,1},{9,13},{13,9},{2,6},{6,2},{1... | collective-permute-start | bytes 6291464 | tf_op jit(solution)/shard_map/ppermute | solution.py:43
  789.0 51.2 %collective-permute-start.44 = (bf16[4096,256]{1,0:T(8,128)(2,1)S(1)}, bf16[4096,256]{1,0:T(8,128)(2,1)S(1)}, u32[]{:S(2)}, u32[]{:S(2)}) collective-permute-start(bf16[4096,256]{1,0:T(8,128)(2,1)S(1)} %collective-permute-done.37.refs_2_), channel_id=1, source_target_pairs={{0,4},{4,0},{8,12},{12,8},{1,5},{5,1},{9,13},{13,9},{2,6},{6,2},{1... | collective-permute-start | bytes 6291464 | tf_op jit(solution)/shard_map/ppermute | solution.py:43
  791.0 51.2 %collective-permute-start.45 = (bf16[4096,256]{1,0:T(8,128)(2,1)S(1)}, bf16[4096,256]{1,0:T(8,128)(2,1)S(1)}, u32[]{:S(2)}, u32[]{:S(2)}) collective-permute-start(bf16[4096,256]{1,0:T(8,128)(2,1)S(1)} %pad_maximum_fusion.8.refs_3_), channel_id=1, source_target_pairs={{0,4},{4,0},{8,12},{12,8},{1,5},{5,1},{9,13},{13,9},{2,6},{6,2},{1... | collective-permute-start | bytes 6291464 | tf_op jit(solution)/shard_map/ppermute | solution.py:43
  835.3 48.7 %collective-permute-start.35 = (bf16[2048,512]{1,0:T(8,128)(2,1)}, bf16[2048,512]{1,0:T(8,128)(2,1)}, u32[]{:S(2)}, u32[]{:S(2)}) collective-permute-start(bf16[2048,512]{1,0:T(8,128)(2,1)} %fusion.28), channel_id=1, source_target_pairs={{0,16},{16,0},{1,17},{17,1},{2,18},{18,2},{3,19},{19,3},{4,20},{20... | collective-permute-start | bytes 6291464 | tf_op jit(solution)/shard_map/ppermute | solution.py:20
  846.1 82.4 %collective-permute-start.47 = (bf16[2048,512]{1,0:T(8,128)(2,1)}, bf16[2048,512]{1,0:T(8,128)(2,1)}, u32[]{:S(2)}, u32[]{:S(2)}) collective-permute-start(bf16[2048,512]{1,0:T(8,128)(2,1)} %fusion.20), channel_id=1, source_target_pairs={{0,16},{16,0},{1,17},{17,1},{2,18},{18,2},{3,19},{19,3},{4,20},{20... | collective-permute-start | bytes 6291464 | tf_op jit(solution)/shard_map/ppermute | solution.py:20
  (65 other events, 1265.2 us)
Sparse Core Ops, SparseCore 0:
  23.1 79.4 reduce-scatter.4
  105.6 104.3 reduce-scatter.6
  212.8 107.8 reduce-scatter.8
  346.3 122.4 reduce-scatter.10

commit v3 on v2

--- a/solution.py
+++ b/solution.py
@@ -25,45 +25,49 @@
     return lax.optimization_barrier((value, earlier))[0]
 
 
-def gather_pairs(block):
-    middle = (lax.axis_index("depth") == 1) | (lax.axis_index("depth") == 2)
-    outer = lax.ppermute(block, "depth", [(0, 1), (1, 0), (2, 3), (3, 2)])
-    inner = lax.ppermute(block, "depth", [(1, 2), (2, 1)])
-    far_inner = lax.ppermute(outer, "depth", [(1, 2), (2, 1)])
-    far_outer = lax.ppermute(inner, "depth", [(2, 3), (1, 0)])
-    last = lax.ppermute(far_inner, "depth", [(2, 3), (1, 0)])
-    near = jnp.concatenate([block, outer], axis=1)
-    far = jnp.concatenate(
-        [jnp.where(middle, inner, far_outer), jnp.where(middle, far_inner, last)], axis=1
-    )
-    held = []
-    for pair in (near, far):
-        other = lax.ppermute(pair, "col", [(0, 2), (1, 3), (2, 0), (3, 1)])
-        held += [pair, other]
-    return (far, held[1]), held + [lax.ppermute(pair, "col", [(0, 1), (1, 0), (2, 3), (3, 2)]) for pair in held]
+def across(block):
+    return lax.ppermute(block, "col", [(0, 2), (1, 3), (2, 0), (3, 1)])
 
 
-def gather(block):
+def gather_pairs(block, earlier):
+    depth_count = lax.axis_size("depth")
+    pair = jnp.concatenate([block, across(block)], axis=1)
+    line = lax.all_gather(block, "depth", axis=0)
+    if earlier:
+        line = after(line, earlier)
+    place = lax.axis_index("depth")
+    rest = jnp.concatenate(
+        [
+            lax.dynamic_index_in_dim(line, (place + k) % depth_count, 0, keepdims=False)
+            for k in range(1, depth_count)
+        ],
+        axis=1,
+    )
+    held = [pair, rest, across(rest)]
+    return held + [lax.ppermute(part, "col", [(0, 1), (1, 0), (2, 3), (3, 2)]) for part in held]
+
+
+def gather(block, earlier):
     sizes = (lax.axis_size("row"), lax.axis_size("col"), lax.axis_size("depth"))
     if sizes == (2, 4, 4):
-        return gather_pairs(block)
-    return block, [lax.all_gather(block, ("col", "depth"), axis=1, tiled=True)]
+        return gather_pairs(block, earlier)
+    return [lax.all_gather(block, ("col", "depth"), axis=1, tiled=True)]
 
 
 def product_tile(summed, *refs):
     *parts, gram, out = refs[1:] if summed else refs
-    width = parts[0].shape[1]
     total = refs[0][...] if summed else None
-    for i, part in enumerate(parts):
-        term = jnp.dot(
-            part[...], gram[i * width : (i + 1) * width, :], preferred_element_type=jnp.float32
-        )
+    start = 0
+    for part in parts:
+        stop = start + part.shape[1]
+        term = jnp.dot(part[...], gram[start:stop, :], preferred_element_type=jnp.float32)
         total = term if total is None else total + term
+        start = stop
     out[...] = total
 
 
 def add_product(running, parts, gram):
-    rows, width = parts[0].shape
+    rows = parts[0].shape[0]
     columns = gram.shape[1]
     tile = min(rows, 256)
     summed = running is not None
@@ -73,7 +77,7 @@
         grid=(rows // tile,),
         out_shape=jax.ShapeDtypeStruct((rows, columns), jnp.float32),
         in_specs=[wide] * summed
-        + [pl.BlockSpec((tile, width), lambda i: (i, 0))] * len(parts)
+        + [pl.BlockSpec((tile, part.shape[1]), lambda i: (i, 0)) for part in parts]
         + [pl.BlockSpec(gram.shape, lambda i: (0, 0))],
         out_specs=wide,
         input_output_aliases={0: 0} if summed else {},
@@ -107,11 +111,10 @@
         sums.append(lax.psum_scatter(scaled, "depth", scatter_dimension=0))
 
     momenta, mine, squares, panels = [], [], [], []
-    relayed = None
     for j in range(PIECES):
         gradient = sums[j]
-        if relayed is not None:
-            gradient = after(gradient, relayed)
+        if mine:
+            gradient, mine[-1] = lax.optimization_barrier((gradient, mine[-1]))
         gradient = gradient.astype(jnp.float32)
         new = BETA * lax.slice_in_dim(momentum, j * width, (j + 1) * width, axis=1) + gradient
         nesterov = gradient + BETA * new
@@ -121,10 +124,10 @@
         momenta.append(new)
         mine.append(kept)
         squares.append(square)
-        relayed, held = gather(kept)
-        if panels:
-            relayed = (relayed, panels[-1])
-        panels.append(held)
+    for j in range(PIECES):
+        earlier = [held[2] for held in panels[-1:] if len(held) > 1]
+        earlier += [held[3:] for held in panels[-2:-1] if len(held) > 1]
+        panels.append(gather(mine[j], earlier))
     total_sq = lax.psum(sum(squares), ("row", "col", "depth"))
     factor = math.sqrt(M) / (1.5 * (jnp.sqrt(total_sq) + EPSILON))
     own = jnp.concatenate(mine, axis=1)

time: 974 us -> 912 us (0.936)
  waiting for transfers between devices: 587 us -> 464 us
  blocking collectives: 44.3 us -> 93 us
  starting transfers between devices: 48.3 us -> 16.7 us
  matrix products: 97.3 us -> 118 us
  local copies, waits for them, and re-layouts: 18.5 us -> 35.7 us
    ppermute x44 -> x20, waiting for transfers between devices: 462 us -> 92.5 us  [the longest x8 92.5 us: across(): return lax.ppermute(block, 'col', [(0, 2), (1, 3), (2, 0), (3, 1)])]
    reduce_scatter x4, waiting for transfers between devices: 71 us -> 292 us  [body(): sums.append(lax.psum_scatter(scaled, 'depth', scatter_dimension=0))]
    psum x1, blocking collectives: 44.3 us -> 93 us  [body(): total_sq = lax.psum(sum(squares), ('row', 'col', 'depth'))]
    ppermute x44 -> x20, starting transfers between devices: 43.9 us -> 13.3 us  [the longest x8 11.1 us: across(): return lax.ppermute(block, 'col', [(0, 2), (1, 3), (2, 0), (3, 1)])]
    dot_general x32 -> x24, matrix products: 97.3 us -> 118 us  [body(): lax.dot_general(part, own, (((0,), (0,)), ((), ())), preferred_element_ty...]
    all_gather x0 -> x4, waiting for transfers between devices: none -> 19.9 us  [gather_pairs(): line = lax.all_gather(block, 'depth', axis=0)]
  transfers between devices with their start and end apart: 52 -> 32, of which waited for: 19 -> 14; matrix products, arithmetic and copies ran while one was open for 16% -> 22% of each run, Pallas kernels for 6% -> 7%
where the time goes in v3:
time: 912 us; the launch traced here: 903 us
  waiting for transfers between devices  464 us (51%)
  matrix products  118 us (13%)
  blocking collectives  93 us (10%)
  Pallas kernels  80.6 us (9%)
  other arithmetic  77.7 us (9%)
  local copies, waits for them, and re-layouts  35.7 us (4%)
  between operations  18 us (2%)
  starting transfers between devices  16.7 us (2%)
    reduce_scatter x4, waiting for transfers between devices, body(): sums.append(lax.psum_scatter(scaled, 'depth', scatter_dimension=0))  292 us
    dot_general x24, matrix products, body(): lax.dot_general(part, own, (((0,), (0,)), ((), ())), preferred_element_ty...  118 us
    psum x1, blocking collectives, body(): total_sq = lax.psum(sum(squares), ('row', 'col', 'depth'))  93 us
    ppermute x8, waiting for transfers between devices, across(): return lax.ppermute(block, 'col', [(0, 2), (1, 3), (2, 0), (3, 1)])  92.5 us
    pallas_call x4, Pallas kernels, add_product(): pl.pallas_call(functools.partial(product_tile, summed), grid=(rows // til...  80.6 us
    ppermute x4, waiting for transfers between devices, row_sum(): moved = lax.ppermute(block.astype(jnp.bfloat16), 'row', [(0, 1), (1, 0)])  59.3 us
    all_gather x4, waiting for transfers between devices, gather_pairs(): line = lax.all_gather(block, 'depth', axis=0)  19.9 us
  transfers between devices with their start and end apart: 32, of which 14 were waited for; matrix products, arithmetic and copies ran while one was open for 22% of the time, Pallas kernels for 7%

profile of v3, /device:TPU:0, one launch (start us, length us, event | category | flops | bytes accessed | tf_op | source)
XLA Modules:
  0.0 902.8 jit_solution(12831808858214480738)
XLA Ops:
  8.1 4.8 fusion.14
  13.0 7.6 fusion.15
  37.0 65.4 %reduce-scatter.5.cloned.1.call-done = bf16[1,4096,128]{2,1,0:T(8,128)(2,1)} async-done(((bf16[4,4096,128]{2,1,0:T(8,128)(2,1)}), bf16[1,4096,128]{2,1,0:T(8,128)(2,1)}) %reduce-scatter.5.cloned.1.call-update) | async-done | bytes 1048592 | tf_op jit(solution)/shard_map/reduce_scatter | solution.py:111
  106.5 75.7 %reduce-scatter.7.cloned.1.call-done = bf16[1,4096,128]{2,1,0:T(8,128)(2,1)} async-done(((bf16[4,4096,128]{2,1,0:T(8,128)(2,1)}), bf16[1,4096,128]{2,1,0:T(8,128)(2,1)}) %reduce-scatter.7.cloned.1.call-update) | async-done | bytes 1048592 | tf_op jit(solution)/shard_map/reduce_scatter | solution.py:111
  182.2 4.9 convert_add_fusion.7
  187.1 75.2 %reduce-scatter.9.cloned.1.call-done = bf16[1,4096,128]{2,1,0:T(8,128)(2,1)} async-done(((bf16[4,4096,128]{2,1,0:T(8,128)(2,1)}), bf16[1,4096,128]{2,1,0:T(8,128)(2,1)}) %reduce-scatter.9.cloned.1.call-update) | async-done | bytes 1048592 | tf_op jit(solution)/shard_map/reduce_scatter | solution.py:111
  262.4 4.8 convert_add_fusion.5
  267.2 75.2 %reduce-scatter.11.cloned.1.call-done = bf16[1,4096,128]{2,1,0:T(8,128)(2,1)} async-done(((bf16[4,4096,128]{2,1,0:T(8,128)(2,1)}), bf16[1,4096,128]{2,1,0:T(8,128)(2,1)}) %reduce-scatter.11.cloned.1.call-update) | async-done | bytes 1048592 | tf_op jit(solution)/shard_map/reduce_scatter | solution.py:111
  353.5 93.0 %psum.7 = f32[]{:T(128)} all-reduce(f32[]{:T(128)S(6)} %add.124), channel_id=1, replica_groups=mesh['row'=2,'col'=4,'depth'=4] {'row','col','depth'}, use_global_device_ids=true, to_apply=%region_8.9 | all-reduce | flops 1 | bytes 8 | tf_op jit(solution)/shard_map/psum | solution.py:131
  461.4 5.7 pad_maximum_fusion
  496.3 9.9 %all-gather.11.cloned.1.call-done = bf16[16384,128]{1,0:T(8,128)(2,1)} async-done(((bf16[4096,128]{1,0:T(8,128)(2,1)}), bf16[16384,128]{1,0:T(8,128)(2,1)}) %all-gather.11.cloned.1.call-update) | async-done | bytes 4194320 | tf_op jit(solution)/shard_map/all_gather | solution.py:35
  506.2 33.8 %collective-permute-done.1.refs_2_ = bf16[4096,384]{1,0:T(8,128)(2,1)S(1)} collective-permute-done((bf16[4096,384]{1,0:T(8,128)(2,1)}, bf16[4096,384]{1,0:T(8,128)(2,1)S(1)}, u32[]{:S(2)}, u32[]{:S(2)}) %collective-permute-start.1) | collective-permute-done | bytes 3145760 | tf_op jit(solution)/shard_map/ppermute | solution.py:29
  551.5 4.9 fusion.35
  571.3 5.7 fusion.33
  577.0 10.0 %all-gather.13.cloned.1.call-done = bf16[16384,128]{1,0:T(8,128)(2,1)} async-done(((bf16[4096,128]{1,0:T(8,128)(2,1)}), bf16[16384,128]{1,0:T(8,128)(2,1)}) %all-gather.13.cloned.1.call-update) | async-done | bytes 4194320 | tf_op jit(solution)/shard_map/all_gather | solution.py:35
  587.0 26.6 %collective-permute-done.7.refs_3_ = bf16[4096,384]{1,0:T(8,128)(2,1)S(1)} collective-permute-done((bf16[4096,384]{1,0:T(8,128)(2,1)}, bf16[4096,384]{1,0:T(8,128)(2,1)S(1)}, u32[]{:S(2)}, u32[]{:S(2)}) %collective-permute-start.7) | collective-permute-done | bytes 3145760 | tf_op jit(solution)/shard_map/ppermute | solution.py:29
  619.5 6.1 fusion.32
  635.7 5.8 fusion.29
  646.2 27.6 %collective-permute-done.5 = bf16[2048,512]{1,0:T(8,128)(2,1)S(1)} collective-permute-done((bf16[2048,512]{1,0:T(8,128)(2,1)}, bf16[2048,512]{1,0:T(8,128)(2,1)S(1)}, u32[]{:S(2)}, u32[]{:S(2)}) %collective-permute-start.5) | collective-permute-done | bytes 2097184 | tf_op jit(solution)/shard_map/ppermute | solution.py:20
  677.4 8.2 collective-permute-done.13.refs_3_
  691.6 19.6 %shard_map.50.refs_0_ = f32[4096,512]{1,0:T(8,128)} custom-call(bf16[4096,256]{1,0:T(8,128)(2,1)} %constant_dynamic-update-slice_fusion.4.refs_0_, bf16[4096,384]{1,0:T(8,128)(2,1)} %pad_maximum_fusion.5.refs_1_, bf16[4096,384]{1,0:T(8,128)(2,1)S(1)} %copy-done.4, bf16[4096,256]{1,0:T(8,128)(2,1)} %collective-permute-done.2.refs_3_, ...), custom_call_target="tpu_custom_call" | custom-call | flops 8589934592 | bytes 33554432 | tf_op jit(solution)/shard_map/pallas_call | solution.py:75
  711.3 5.7 fusion.28
  717.7 5.7 fusion.26
  732.8 23.9 %collective-permute-done.19.refs_3_ = bf16[4096,384]{1,0:T(8,128)(2,1)S(1)} collective-permute-done((bf16[4096,384]{1,0:T(8,128)(2,1)}, bf16[4096,384]{1,0:T(8,128)(2,1)S(1)}, u32[]{:S(2)}, u32[]{:S(2)}) %collective-permute-start.19) | collective-permute-done | bytes 3145760 | tf_op jit(solution)/shard_map/ppermute | solution.py:29
  756.8 5.7 fusion.25
  784.5 5.1 fusion.20
  791.2 20.8 %shard_map.51.refs_0_ = f32[4096,512]{1,0:T(8,128)} custom-call(f32[4096,512]{1,0:T(8,128)} %shard_map.50.refs_0_, bf16[4096,256]{1,0:T(8,128)(2,1)} %constant_dynamic-update-slice_fusion.6.refs_1_, bf16[4096,384]{1,0:T(8,128)(2,1)} %pad_maximum_fusion.6.refs_2_, ...), custom_call_target="tpu_custom_call", output_to_operand_aliasing={{}: (0, {})} | custom-call | flops 8589934592 | bytes 33554432 | tf_op jit(solution)/shard_map/pallas_call | solution.py:75
  812.0 9.1 %collective-permute-done.17 = bf16[2048,512]{1,0:T(8,128)(2,1)} collective-permute-done((bf16[2048,512]{1,0:T(8,128)(2,1)}, bf16[2048,512]{1,0:T(8,128)(2,1)}, u32[]{:S(2)}, u32[]{:S(2)}) %collective-permute-start.17) | collective-permute-done | bytes 2097184 | tf_op jit(solution)/shard_map/ppermute | solution.py:20
  823.9 20.9 %shard_map.52.refs_0_ = f32[4096,512]{1,0:T(8,128)} custom-call(f32[4096,512]{1,0:T(8,128)} %shard_map.51.refs_0_, bf16[4096,256]{1,0:T(8,128)(2,1)} %constant_dynamic-update-slice_fusion.8.refs_1_, bf16[4096,384]{1,0:T(8,128)(2,1)} %pad_maximum_fusion.7.refs_2_, bf16[4096,384]{1,0:T(8,128)(2,1)} %collective-permute-done.13.refs_3_, ...), custom_call_target="tpu_custom_call", output_to_operand_aliasing={{}: (0, {})} | custom-call | flops 8589934592 | bytes 33554432 | tf_op jit(solution)/shard_map/pallas_call | solution.py:75
  844.8 19.9 %collective-permute-done.23 = bf16[2048,512]{1,0:T(8,128)(2,1)} collective-permute-done((bf16[2048,512]{1,0:T(8,128)(2,1)S(1)}, bf16[2048,512]{1,0:T(8,128)(2,1)}, u32[]{:S(2)}, u32[]{:S(2)}) %collective-permute-start.23) | collective-permute-done | bytes 2097184 | tf_op jit(solution)/shard_map/ppermute | solution.py:20
  867.0 19.3 %shard_map.53 = f32[4096,512]{1,0:T(8,128)} custom-call(f32[4096,512]{1,0:T(8,128)} %shard_map.52.refs_0_, bf16[4096,256]{1,0:T(8,128)(2,1)} %constant_dynamic-update-slice_fusion.10.refs_1_, bf16[4096,384]{1,0:T(8,128)(2,1)} %pad_maximum_fusion.8.refs_2_, bf16[4096,384]{1,0:T(8,128)(2,1)S(1)} %collective-permute-done.19.refs_3_, ...), custom_call_target="tpu_custom_call", output_to_operand_aliasing={{}: (0, {})} | custom-call | flops 8589934592 | bytes 33554432 | tf_op jit(solution)/shard_map/pallas_call | solution.py:75
  886.3 9.5 %subtract_multiply_fusion = f32[4096,512]{1,0:T(8,128)} fusion(f32[4096,512]{1,0:T(8,128)} %shard_map.53, bf16[4096,512]{1,0:T(8,128)(2,1)} %get-tuple-element.77, f32[]{:T(128)S(6)} %mul.321), kind=kLoop, calls=%fused_computation.1 | loop fusion | flops 10485760 | bytes 20971524 | tf_op jit(solution)/shard_map/mul | solution.py:150
  (140 shorter events, 168.4 us)
Async XLA Ops:
  7.2 95.3 %reduce-scatter.5.cloned.1.call-start = ((), (), s32[]{:S(2)}) async-start(), calls=%async_computation.4 | async-start | bytes 5242880 | tf_op jit(solution)/shard_map/reduce_scatter | solution.py:111
  22.8 159.3 %reduce-scatter.7.cloned.1.call-start = ((), (), s32[]{:S(2)}) async-start(), calls=%async_computation.5 | async-start | bytes 5242880 | tf_op jit(solution)/shard_map/reduce_scatter | solution.py:111
  26.2 236.1 %reduce-scatter.9.cloned.1.call-start = ((), (), s32[]{:S(2)}) async-start(), calls=%async_computation.6 | async-start | bytes 5242880 | tf_op jit(solution)/shard_map/reduce_scatter | solution.py:111
  31.4 311.1 %reduce-scatter.11.cloned.1.call-start = ((), (), s32[]{:S(2)}) async-start(), calls=%async_computation.7 | async-start | bytes 5242880 | tf_op jit(solution)/shard_map/reduce_scatter | solution.py:111
  37.0 430.2 %all-gather.9.cloned.1.call-start = ((), (), s32[]{:S(2)}) async-start(), calls=%async_computation.8 | async-start | bytes 5242880 | tf_op jit(solution)/shard_map/all_gather | solution.py:35
  182.2 324.0 %all-gather.11.cloned.1.call-start = ((), (), s32[]{:S(2)}) async-start(), calls=%async_computation.9 | async-start | bytes 5242880 | tf_op jit(solution)/shard_map/all_gather | solution.py:35
  262.4 324.6 %all-gather.13.cloned.1.call-start = ((), (), s32[]{:S(2)}) async-start(), calls=%async_computation.10 | async-start | bytes 5242880 | tf_op jit(solution)/shard_map/all_gather | solution.py:35
  342.5 335.0 %all-gather.15.cloned.1.call-start = ((), (), s32[]{:S(2)}) async-start(), calls=%async_computation.11 | async-start | bytes 5242880 | tf_op jit(solution)/shard_map/all_gather | solution.py:35
  342.6 129.4 %collective-permute-start = (bf16[4096,128]{1,0:T(8,128)(2,1)}, bf16[4096,128]{1,0:T(8,128)(2,1)}, u32[]{:S(2)}, u32[]{:S(2)}) collective-permute-start(bf16[4096,128]{1,0:T(8,128)(2,1)} %get-tuple-element.29), channel_id=1, source_target_pairs={{0,8},{4,12},{8,0},{12,4},{1,9},{5,13},{9,1},{13,5},{2,10},{6,14},... | collective-permute-start | bytes 3145736 | tf_op jit(solution)/shard_map/ppermute | solution.py:29
  344.1 130.2 %collective-permute-start.6 = (bf16[4096,128]{1,0:T(8,128)(2,1)}, bf16[4096,128]{1,0:T(8,128)(2,1)}, u32[]{:S(2)}, u32[]{:S(2)}) collective-permute-start(bf16[4096,128]{1,0:T(8,128)(2,1)} %get-tuple-element.30), channel_id=1, source_target_pairs={{0,8},{4,12},{8,0},{12,4},{1,9},{5,13},{9,1},{13,5},{2,10},{6,14},... | collective-permute-start | bytes 3145736 | tf_op jit(solution)/shard_map/ppermute | solution.py:29
  351.9 125.2 %collective-permute-start.12 = (bf16[4096,128]{1,0:T(8,128)(2,1)}, bf16[4096,128]{1,0:T(8,128)(2,1)}, u32[]{:S(2)}, u32[]{:S(2)}) collective-permute-start(bf16[4096,128]{1,0:T(8,128)(2,1)} %get-tuple-element.31), channel_id=1, source_target_pairs={{0,8},{4,12},{8,0},{12,4},{1,9},{5,13},{9,1},{13,5},{2,10},{6,14},... | collective-permute-start | bytes 3145736 | tf_op jit(solution)/shard_map/ppermute | solution.py:29
  447.2 32.3 %collective-permute-start.18 = (bf16[4096,128]{1,0:T(8,128)(2,1)}, bf16[4096,128]{1,0:T(8,128)(2,1)}, u32[]{:S(2)}, u32[]{:S(2)}) collective-permute-start(bf16[4096,128]{1,0:T(8,128)(2,1)} %get-tuple-element.32), channel_id=1, source_target_pairs={{0,8},{4,12},{8,0},{12,4},{1,9},{5,13},{9,1},{13,5},{2,10},{6,14},... | collective-permute-start | bytes 3145736 | tf_op jit(solution)/shard_map/ppermute | solution.py:29
  472.0 68.0 %collective-permute-start.1 = (bf16[4096,384]{1,0:T(8,128)(2,1)}, bf16[4096,384]{1,0:T(8,128)(2,1)S(1)}, u32[]{:S(2)}, u32[]{:S(2)}) collective-permute-start(bf16[4096,384]{1,0:T(8,128)(2,1)} %pad_maximum_fusion.5.refs_1_), channel_id=1, source_target_pairs={{0,8},{4,12},{8,0},{12,4},{1,9},{5,13},{9,1},{13,5},{2,10},{6,14},... | collective-permute-start | bytes 9437192 | tf_op jit(solution)/shard_map/ppermute | solution.py:29
  474.3 86.9 %collective-permute-start.2 = (bf16[4096,256]{1,0:T(8,128)(2,1)}, bf16[4096,256]{1,0:T(8,128)(2,1)}, u32[]{:S(2)}, u32[]{:S(2)}) collective-permute-start(bf16[4096,256]{1,0:T(8,128)(2,1)} %constant_dynamic-update-slice_fusion.4.refs_0_), channel_id=1, source_target_pairs={{0,4},{4,0},{8,12},{12,8},{1,5},{5,1},{9,13},{13,9},{2,6},{6,2},{1... | collective-permute-start | bytes 6291464 | tf_op jit(solution)/shard_map/ppermute | solution.py:47
  476.6 153.8 %collective-permute-start.8 = (bf16[4096,256]{1,0:T(8,128)(2,1)}, bf16[4096,256]{1,0:T(8,128)(2,1)}, u32[]{:S(2)}, u32[]{:S(2)}) collective-permute-start(bf16[4096,256]{1,0:T(8,128)(2,1)} %constant_dynamic-update-slice_fusion.6.refs_1_), channel_id=1, source_target_pairs={{0,4},{4,0},{8,12},{12,8},{1,5},{5,1},{9,13},{13,9},{2,6},{6,2},{1... | collective-permute-start | bytes 6291464 | tf_op jit(solution)/shard_map/ppermute | solution.py:47
  496.2 75.0 %collective-permute-start.3 = (bf16[4096,384]{1,0:T(8,128)(2,1)}, bf16[4096,384]{1,0:T(8,128)(2,1)}, u32[]{:S(2)}, u32[]{:S(2)}) collective-permute-start(bf16[4096,384]{1,0:T(8,128)(2,1)} %pad_maximum_fusion.5.refs_1_), channel_id=1, source_target_pairs={{0,4},{4,0},{8,12},{12,8},{1,5},{5,1},{9,13},{13,9},{2,6},{6,2},{1... | collective-permute-start | bytes 9437192 | tf_op jit(solution)/shard_map/ppermute | solution.py:47
  545.2 68.4 %collective-permute-start.7 = (bf16[4096,384]{1,0:T(8,128)(2,1)}, bf16[4096,384]{1,0:T(8,128)(2,1)S(1)}, u32[]{:S(2)}, u32[]{:S(2)}) collective-permute-start(bf16[4096,384]{1,0:T(8,128)(2,1)} %pad_maximum_fusion.6.refs_2_), channel_id=1, source_target_pairs={{0,8},{4,12},{8,0},{12,4},{1,9},{5,13},{9,1},{13,5},{2,10},{6,14},... | collective-permute-start | bytes 9437192 | tf_op jit(solution)/shard_map/ppermute | solution.py:29
  546.7 40.3 %collective-permute-start.4 = (bf16[4096,384]{1,0:T(8,128)(2,1)}, bf16[4096,384]{1,0:T(8,128)(2,1)}, u32[]{:S(2)}, u32[]{:S(2)}) collective-permute-start(bf16[4096,384]{1,0:T(8,128)(2,1)} %copy-done.2), channel_id=1, source_target_pairs={{0,4},{4,0},{8,12},{12,8},{1,5},{5,1},{9,13},{13,9},{2,6},{6,2},{1... | collective-permute-start | bytes 9437192 | tf_op jit(solution)/shard_map/ppermute | solution.py:47
  561.2 74.5 %collective-permute-start.9 = (bf16[4096,384]{1,0:T(8,128)(2,1)}, bf16[4096,384]{1,0:T(8,128)(2,1)}, u32[]{:S(2)}, u32[]{:S(2)}) collective-permute-start(bf16[4096,384]{1,0:T(8,128)(2,1)} %pad_maximum_fusion.6.refs_2_), channel_id=1, source_target_pairs={{0,4},{4,0},{8,12},{12,8},{1,5},{5,1},{9,13},{13,9},{2,6},{6,2},{1... | collective-permute-start | bytes 9437192 | tf_op jit(solution)/shard_map/ppermute | solution.py:47
  617.7 67.9 %collective-permute-start.13 = (bf16[4096,384]{1,0:T(8,128)(2,1)}, bf16[4096,384]{1,0:T(8,128)(2,1)}, u32[]{:S(2)}, u32[]{:S(2)}) collective-permute-start(bf16[4096,384]{1,0:T(8,128)(2,1)} %pad_maximum_fusion.7.refs_2_), channel_id=1, source_target_pairs={{0,8},{4,12},{8,0},{12,4},{1,9},{5,13},{9,1},{13,5},{2,10},{6,14},... | collective-permute-start | bytes 9437192 | tf_op jit(solution)/shard_map/ppermute | solution.py:29
  619.5 58.0 %collective-permute-start.10 = (bf16[4096,384]{1,0:T(8,128)(2,1)S(1)}, bf16[4096,384]{1,0:T(8,128)(2,1)}, u32[]{:S(2)}, u32[]{:S(2)}) collective-permute-start(bf16[4096,384]{1,0:T(8,128)(2,1)S(1)} %collective-permute-done.7.refs_3_), channel_id=1, source_target_pairs={{0,4},{4,0},{8,12},{12,8},{1,5},{5,1},{9,13},{13,9},{2,6},{6,2},{1... | collective-permute-start | bytes 9437192 | tf_op jit(solution)/shard_map/ppermute | solution.py:47
  625.6 48.2 %collective-permute-start.5 = (bf16[2048,512]{1,0:T(8,128)(2,1)}, bf16[2048,512]{1,0:T(8,128)(2,1)S(1)}, u32[]{:S(2)}, u32[]{:S(2)}) collective-permute-start(bf16[2048,512]{1,0:T(8,128)(2,1)} %fusion.32), channel_id=1, source_target_pairs={{0,16},{16,0},{1,17},{17,1},{2,18},{18,2},{3,19},{19,3},{4,20},{20... | collective-permute-start | bytes 6291464 | tf_op jit(solution)/shard_map/ppermute | solution.py:20
  630.4 97.1 %collective-permute-start.14 = (bf16[4096,256]{1,0:T(8,128)(2,1)}, bf16[4096,256]{1,0:T(8,128)(2,1)}, u32[]{:S(2)}, u32[]{:S(2)}) collective-permute-start(bf16[4096,256]{1,0:T(8,128)(2,1)} %constant_dynamic-update-slice_fusion.8.refs_1_), channel_id=1, source_target_pairs={{0,4},{4,0},{8,12},{12,8},{1,5},{5,1},{9,13},{13,9},{2,6},{6,2},{1... | collective-permute-start | bytes 6291464 | tf_op jit(solution)/shard_map/ppermute | solution.py:47
  635.7 97.0 %collective-permute-start.15 = (bf16[4096,384]{1,0:T(8,128)(2,1)}, bf16[4096,384]{1,0:T(8,128)(2,1)}, u32[]{:S(2)}, u32[]{:S(2)}) collective-permute-start(bf16[4096,384]{1,0:T(8,128)(2,1)} %pad_maximum_fusion.7.refs_2_), channel_id=1, source_target_pairs={{0,4},{4,0},{8,12},{12,8},{1,5},{5,1},{9,13},{13,9},{2,6},{6,2},{1... | collective-permute-start | bytes 9437192 | tf_op jit(solution)/shard_map/ppermute | solution.py:47
  689.9 66.9 %collective-permute-start.19 = (bf16[4096,384]{1,0:T(8,128)(2,1)}, bf16[4096,384]{1,0:T(8,128)(2,1)S(1)}, u32[]{:S(2)}, u32[]{:S(2)}) collective-permute-start(bf16[4096,384]{1,0:T(8,128)(2,1)} %pad_maximum_fusion.8.refs_2_), channel_id=1, source_target_pairs={{0,8},{4,12},{8,0},{12,4},{1,9},{5,13},{9,1},{13,5},{2,10},{6,14},... | collective-permute-start | bytes 9437192 | tf_op jit(solution)/shard_map/ppermute | solution.py:29
  711.2 56.3 %collective-permute-start.16 = (bf16[4096,384]{1,0:T(8,128)(2,1)}, bf16[4096,384]{1,0:T(8,128)(2,1)S(1)}, u32[]{:S(2)}, u32[]{:S(2)}) collective-permute-start(bf16[4096,384]{1,0:T(8,128)(2,1)} %collective-permute-done.13.refs_3_), channel_id=1, source_target_pairs={{0,4},{4,0},{8,12},{12,8},{1,5},{5,1},{9,13},{13,9},{2,6},{6,2},{1... | collective-permute-start | bytes 9437192 | tf_op jit(solution)/shard_map/ppermute | solution.py:47
  717.0 48.2 %collective-permute-start.11 = (bf16[2048,512]{1,0:T(8,128)(2,1)}, bf16[2048,512]{1,0:T(8,128)(2,1)S(1)}, u32[]{:S(2)}, u32[]{:S(2)}) collective-permute-start(bf16[2048,512]{1,0:T(8,128)(2,1)} %fusion.28), channel_id=1, source_target_pairs={{0,16},{16,0},{1,17},{17,1},{2,18},{18,2},{3,19},{19,3},{4,20},{20... | collective-permute-start | bytes 6291464 | tf_op jit(solution)/shard_map/ppermute | solution.py:20
  727.5 53.0 %collective-permute-start.21 = (bf16[4096,384]{1,0:T(8,128)(2,1)}, bf16[4096,384]{1,0:T(8,128)(2,1)S(1)}, u32[]{:S(2)}, u32[]{:S(2)}) collective-permute-start(bf16[4096,384]{1,0:T(8,128)(2,1)} %pad_maximum_fusion.8.refs_2_), channel_id=1, source_target_pairs={{0,4},{4,0},{8,12},{12,8},{1,5},{5,1},{9,13},{13,9},{2,6},{6,2},{1... | collective-permute-start | bytes 9437192 | tf_op jit(solution)/shard_map/ppermute | solution.py:47
  732.7 44.3 %collective-permute-start.20 = (bf16[4096,256]{1,0:T(8,128)(2,1)}, bf16[4096,256]{1,0:T(8,128)(2,1)S(1)}, u32[]{:S(2)}, u32[]{:S(2)}) collective-permute-start(bf16[4096,256]{1,0:T(8,128)(2,1)} %constant_dynamic-update-slice_fusion.10.refs_1_), channel_id=1, source_target_pairs={{0,4},{4,0},{8,12},{12,8},{1,5},{5,1},{9,13},{13,9},{2,6},{6,2},{1... | collective-permute-start | bytes 6291464 | tf_op jit(solution)/shard_map/ppermute | solution.py:47
  756.8 27.7 %collective-permute-start.22 = (bf16[4096,384]{1,0:T(8,128)(2,1)S(1)}, bf16[4096,384]{1,0:T(8,128)(2,1)S(1)}, u32[]{:S(2)}, u32[]{:S(2)}) collective-permute-start(bf16[4096,384]{1,0:T(8,128)(2,1)S(1)} %collective-permute-done.19.refs_3_), channel_id=1, source_target_pairs={{0,4},{4,0},{8,12},{12,8},{1,5},{5,1},{9,13},{13,9},{2,6},{6,2},{1... | collective-permute-start | bytes 9437192 | tf_op jit(solution)/shard_map/ppermute | solution.py:47
  772.2 48.8 %collective-permute-start.17 = (bf16[2048,512]{1,0:T(8,128)(2,1)}, bf16[2048,512]{1,0:T(8,128)(2,1)}, u32[]{:S(2)}, u32[]{:S(2)}) collective-permute-start(bf16[2048,512]{1,0:T(8,128)(2,1)} %fusion.24), channel_id=1, source_target_pairs={{0,16},{16,0},{1,17},{17,1},{2,18},{18,2},{3,19},{19,3},{4,20},{20... | collective-permute-start | bytes 6291464 | tf_op jit(solution)/shard_map/ppermute | solution.py:20
  789.6 75.1 %collective-permute-start.23 = (bf16[2048,512]{1,0:T(8,128)(2,1)S(1)}, bf16[2048,512]{1,0:T(8,128)(2,1)}, u32[]{:S(2)}, u32[]{:S(2)}) collective-permute-start(bf16[2048,512]{1,0:T(8,128)(2,1)S(1)} %fusion.20), channel_id=1, source_target_pairs={{0,16},{16,0},{1,17},{17,1},{2,18},{18,2},{3,19},{19,3},{4,20},{20... | collective-permute-start | bytes 6291464 | tf_op jit(solution)/shard_map/ppermute | solution.py:20
  (19 other events, 86.5 us)
Sparse Core Ops, SparseCore 0:
  23.0 79.4 reduce-scatter.4
  104.9 77.2 reduce-scatter.6
  185.0 77.2 reduce-scatter.8
  265.2 77.2 reduce-scatter.10
  343.9 81.4 all-gather.8
  426.8 79.3 all-gather.10
  507.8 79.1 all-gather.12
  588.6 79.2 all-gather.14
